TPU v7x, 32 devices: a whole 2x2x4 slice. The times are simulated.
32 devices in a mesh: ens: 2 (over x), space: 8 (over z, y), tm: 2 (over core).
Axes of the slice: x: 2, y: 2, z: 4, core: 2. Of those that a mesh axis runs over, the one named last changes fastest.
Arguments:
- adjoint_in: float32 [4, 3, 3, 64, 2048], P(('ens', 'tm'), None, None, 'space'), parts along dimension 0, may hold values from -6 to 6
- layer_depth: float32 [3, 64, 2048], P(None, 'space'), may hold values from 0.5 to 2
- obs_cell: int32 [4, 131072], P(('ens', 'tm'), 'space'), parts along dimension 0, may hold values from 0 to 16383
- obs_plane: int32 [4, 131072], P(('ens', 'tm'), 'space'), parts along dimension 0, may hold values from 0 to 11
- obs_owner: int32 [4, 131072, 1], P(('ens', 'tm'), 'space'), parts along dimension 0, may hold values from 0 to 7; in each aligned block of 16384 rows (0 to 16383, 16384 to 32767, ..., all dimensions but the last counted through in order) at most 2560 rows name the same one
- innovation: float32 [4, 131072], P(('ens', 'tm'), 'space'), parts along dimension 0, may hold values from -6 to 6
- obs_weight: float32 [4, 4, 131072], P(None, ('ens', 'tm'), 'space'), parts along dimension 1, may hold values from 0 to 1
- obs_count: int32 [4, 8], P(('ens', 'tm'), 'space'), parts along dimension 0, may hold values from 1 to 16384, 98304 in all within a row
Outputs:
- adjoint_out: float32 [4, 3, 3, 64, 2048], P(('ens', 'tm'), None, None, 'space'), parts along dimension 0
There are 2 independent parts, one for each index of `ens`. A program takes and returns all parts, laid end to end along the dimension named above; an argument that names none is the same for every part. Nothing has to cross between parts.
Inputs may be any that keep to these rules, and one draw needn't show every extreme that they name: `obs_owner`: among the 16384 rows of one tile in one sub-window at most 2560 name the same owner tile; some owner is named by exactly 2560 of them. `obs_cell`: the cell lies inside the owner tile; its lower and right neighbours may lie in the next tile or wrap around. `obs_count`: the live rows of a tile are its first ones; the counts of one sub-window sum to 98304 and the largest is 16384.
All inputs are finite; a program needn't handle non-finite values. No bound on the sum of `obs_count` on one device may be relied on, other than what follows from the above.
Results may differ from a plain program's by a relative error of at most 0.000037.
Values sent between devices are 32-bit elements; how exact they have to be, the bound alone decides.
A program may use at most 64 MiB of HBM per device.

v0:
```python
import jax
import jax.numpy as jnp
from jax import lax
from jax.sharding import PartitionSpec as P

STEPS = 4


time_step = 0.4
friction = 0.05
coriolis_mid = 0.3
coriolis_slope = 0.2
coupling = ((1.0, 0.5, 0.25), (0.5, 1.0, 0.5), (0.25, 0.5, 1.0))


def shifted(block, axis, distance):
    devices = range(lax.axis_size(axis))
    route = [(i - distance, i) for i in devices if i - distance in devices]
    return lax.ppermute(block, axis, route)


def shifted_2(block, axis, distance):
    devices = range(lax.axis_size(axis))
    route = [((i - distance) % len(devices), i) for i in devices]
    return lax.ppermute(block, axis, route)


def padded(block, sides, width):
    for axis, dim in sides:
        count = lax.axis_size(axis)
        forward = [(i, i + 1) for i in range(count - 1)]
        forward.append((count - 1, 0))
        backward = [(target, source) for source, target in forward]
        low = lax.ppermute(
            lax.slice_in_dim(block, block.shape[dim] - width, None, axis=dim), axis, forward
        )
        high = lax.ppermute(lax.slice_in_dim(block, 0, width, axis=dim), axis, backward)
        block = jnp.concatenate([low, block, high], axis=dim)
    return block


def couple_layers(field):
    return jnp.stack(
        [
            coupling[0][m] * field[0] + coupling[1][m] * field[1] + coupling[2][m] * field[2]
            for m in range(3)
        ]
    )


def along_rows(field):
    return (field[:, 2:] - field[:, :-2]) * 0.5


def along_cols(field):
    interior = field[:, 1:-1]
    return (jnp.roll(interior, -1, axis=2) - jnp.roll(interior, 1, axis=2)) * 0.5


def advance(extended, depth_ext, coriolis, layer_count):
    height = extended[0:layer_count]
    east = extended[layer_count : 2 * layer_count]
    north = extended[2 * layer_count : 3 * layer_count]
    thick = depth_ext * height
    east_mix = couple_layers(east)
    north_mix = couple_layers(north)
    height_in = height[:, 1:-1]
    east_in = east[:, 1:-1]
    north_in = north[:, 1:-1]
    new_height = height_in + time_step * (along_rows(east_mix) + along_cols(north_mix))
    new_east = east_in + time_step * (along_rows(thick) - coriolis * north_in - friction * east_in)
    new_north = north_in + time_step * (
        along_cols(thick) + coriolis * east_in - friction * north_in
    )
    return jnp.concatenate([new_height, new_east, new_north], axis=0)


def body(
    adjoint_in, layer_depth, obs_cell, obs_plane, obs_owner, innovation, obs_weight, obs_count
):
    tiles = lax.axis_size("space")
    layer_count = layer_depth.shape[0]
    tile_rows = layer_depth.shape[1]
    columns = layer_depth.shape[2]
    obs_rows = obs_cell.shape[1]
    capacity = 5 * obs_rows // (4 * tiles)
    planes = STEPS * layer_count
    following = shifted(adjoint_in, "tm", -1)
    is_live = jnp.arange(obs_rows, dtype=jnp.int32) < obs_count[0, 0]
    owner_tile = obs_owner[0, :, 0]
    target = jnp.where(is_live, owner_tile, tiles)
    owner_hits = (jnp.arange(tiles, dtype=jnp.int32)[:, None] == target[None, :]).astype(jnp.int32)
    running = jnp.cumsum(owner_hits, axis=1)
    slot_rank = jnp.where(is_live, jnp.sum(owner_hits * running, axis=0) - 1, 0)
    position = target * capacity + slot_rank
    cell_float = obs_cell[0].astype(jnp.float32)
    plane_float = obs_plane[0].astype(jnp.float32)
    innov_rows = innovation[0]
    weights = obs_weight[:, 0, :]
    fields = jnp.concatenate(
        [cell_float[None], plane_float[None], innov_rows[None], weights], axis=0
    )
    buffer = jnp.zeros((7, tiles * capacity), jnp.float32).at[:, position].set(fields, mode="drop")
    arrived = lax.all_to_all(
        buffer.reshape(7, tiles, capacity), "space", split_axis=1, concat_axis=1, tiled=True
    )
    arrived = arrived.reshape(7, tiles * capacity)
    corner_values = arrived[3:7] * arrived[2][None]
    cell_index = arrived[0].astype(jnp.int32)
    plane = arrived[1].astype(jnp.int32)
    grid_row = cell_index // columns
    column = cell_index % columns
    next_col = (column + 1) % columns
    forcing = jnp.zeros((planes, tile_rows + 1, columns), jnp.float32)
    forcing = forcing.at[plane, grid_row, column].add(corner_values[0])
    forcing = forcing.at[plane, grid_row, next_col].add(corner_values[1])
    forcing = forcing.at[plane, grid_row + 1, column].add(corner_values[2])
    forcing = forcing.at[plane, grid_row + 1, next_col].add(corner_values[3])
    carried = shifted_2(forcing[:, tile_rows, :], "space", 1)
    forcing = forcing[:, :tile_rows, :].at[:, 0, :].add(carried)
    coriolis = coriolis_mid + coriolis_slope * (
        jnp.arange(columns, dtype=jnp.float32) / columns - 0.5
    )
    adjoint = following[0].reshape(3 * layer_count, tile_rows, columns)
    depth_ext = padded(layer_depth, (("space", 1),), 1)
    current = adjoint
    for step_index in reversed(range(STEPS)):
        current = current.at[0:layer_count].add(
            forcing[step_index * layer_count : (step_index + 1) * layer_count]
        )
        extended = padded(current, (("space", 1),), 1)
        current = advance(extended, depth_ext, coriolis, layer_count)
    result = adjoint_in[0] - current.reshape(3, layer_count, tile_rows, columns)
    return result[None]


def solution(mesh):
    in_specs = (
        P(("ens", "tm"), None, None, "space", None),
        P(None, "space", None),
        P(("ens", "tm"), "space"),
        P(("ens", "tm"), "space"),
        P(("ens", "tm"), "space", None),
        P(("ens", "tm"), "space"),
        P(None, ("ens", "tm"), "space"),
        P(("ens", "tm"), "space"),
    )
    out_specs = P(("ens", "tm"), None, None, "space", None)
    return jax.shard_map(body, mesh=mesh, in_specs=in_specs, out_specs=out_specs, check_vma=False)
```

profile of v0, /device:TPU:0, one launch (start us, length us, event | category | flops | bytes accessed | tf_op | source)
XLA Modules:
  0.0 670.0 jit_solution(11216005782721556500)
XLA Ops:
  0.7 0.9 copy.32
  2.4 1.1 copy.50
  3.5 0.9 convert_element_type.51
  4.4 0.9 convert_element_type.52
  5.3 1.1 maximum_bitcast_fusion
  6.4 5.4 copy.34
  11.9 45.3 %scatter_custom_fusion = f32[7,20480]{0,1:T(8,128)} fusion(s32[16384]{0:T(1024)S(1)} %bitcast.54, f32[16384,7]{1,0:T(8,128)} %copy.34, f32[]{:T(128)} %constant.173.clone.1), kind=kCustom, calls=%fused_computation.5 | custom fusion | bytes 573952 | tf_op jit(solution)/shard_map/scatter | solution.py:103
  57.3 6.8 %copy.35 = f32[7,8,2560]{2,0,1:T(8,128)} copy(f32[7,8,2560]{0,2,1:T(8,128)} %bitcast.37) | data formatting | bytes 1146880 | tf_op jit(solution)/shard_map/reshape | solution.py:105
  64.0 7.3 %all-to-all-start = ((f32[7,8,2560]{2,0,1:T(8,128)}), f32[7,8,2560]{2,0,1:T(8,128)S(1)}, u32[]{:S(2)}, u32[]{:S(2)}) async-start(f32[7,8,2560]{2,0,1:T(8,128)} %copy.35), calls=%async_computation | async-start | bytes 1310720 | tf_op jit(solution)/shard_map/all_to_all | solution.py:104
  71.3 1.3 collective-permute-start
  72.7 2.1 collective-permute-start.4
  74.8 2.8 collective-permute-start.5
  77.6 10.1 %collective-permute-done.4 = f32[3,1,2048]{2,0,1:T(4,128)S(1)} collective-permute-done((f32[3,1,2048]{2,0,1:T(4,128)S(1)}, f32[3,1,2048]{2,0,1:T(4,128)S(1)}, u32[]{:S(2)}, u32[]{:S(2)}) %collective-permute-start.4) | collective-permute-done | bytes 24608 | tf_op jit(solution)/shard_map/ppermute | solution.py:34
  87.7 1.3 all-to-all-done
  89.1 0.4 compare_select_fusion.3
  90.3 1.2 multiply_reduce_fusion
  91.5 1.5 and_reduce_fusion
  93.5 116.7 %scatter_custom_fusion.1 = f32[221184]{0:T(1024)S(1)} fusion(s32[20480]{0:T(1024)S(1)} %broadcast_select_fusion.3, f32[20480]{0:T(1024)S(1)} %bitcast.53, f32[]{:T(128)} %constant.173.clone.1), kind=kCustom, calls=%fused_computation.21 | custom fusion | flops 20480 | bytes 884740
  210.2 118.7 %scatter_fusion = f32[221184]{0:T(1024)S(1)} fusion(f32[221184]{0:T(1024)S(1)} %scatter_custom_fusion.1, s32[20480]{0:T(1024)S(1)} %broadcast_select_fusion.2, f32[20480]{0:T(1024)S(1)} %bitcast.47), kind=kCustom, calls=%fused_computation.2 | custom fusion | flops 20480 | bytes 327680
  328.9 118.5 %scatter_fusion.1 = f32[221184]{0:T(1024)S(1)} fusion(f32[221184]{0:T(1024)S(1)} %scatter_fusion, s32[20480]{0:T(1024)S(1)} %broadcast_select_fusion.1, f32[20480]{0:T(1024)S(1)} %bitcast.46), kind=kCustom, calls=%fused_computation.3 | custom fusion | flops 20480 | bytes 327680
  447.4 118.5 %scatter_fusion.2 = f32[221184]{0:T(1024)S(1)} fusion(f32[221184]{0:T(1024)S(1)} %scatter_fusion.1, s32[20480]{0:T(1024)S(1)} %broadcast_select_fusion, f32[20480]{0:T(1024)S(1)} %bitcast.45), kind=kCustom, calls=%fused_computation.4 | custom fusion | flops 20480 | bytes 327680
  566.8 7.0 %collective-permute-done.1 = f32[12,2048]{1,0:T(8,128)S(1)} collective-permute-done((f32[12,2048]{1,0:T(8,128)S(1)}, f32[12,2048]{1,0:T(8,128)S(1)}, u32[]{:S(2)}, u32[]{:S(2)}) %collective-permute-start.1) | collective-permute-done | bytes 98336 | tf_op jit(solution)/shard_map/ppermute | solution.py:25
  573.8 1.0 copy-done
  574.9 0.8 scatter-add.58
  575.8 43.3 %collective-permute-start.2 = (f32[9,1,2048]{2,0,1:T(8,128)S(1)}, f32[9,1,2048]{2,0,1:T(8,128)S(1)}, u32[]{:S(2)}, u32[]{:S(2)}) collective-permute-start(f32[9,1,2048]{2,0,1:T(8,128)S(1)} %get-tuple-element.146), channel_id=1, source_target_pairs={{0,2},{2,4},{4,6},{6,8},{8,10},{10,12},{12,14},{14,0},{1,3},{3,5},... | collective-permute-start | bytes 221192 | tf_op jit(solution)/shard_map/ppermute | solution.py:34
  619.0 2.5 collective-permute-done.2
  621.5 3.8 collective-permute-done.3
  625.7 0.5 multiply_add_fusion.15
  627.2 0.4 slice_add_fusion.2
  627.7 0.4 fusion.47
  628.3 0.8 scatter-add.59
  629.2 3.1 collective-permute-start.6
  632.2 1.7 collective-permute-start.7
  633.9 3.0 collective-permute-done.6
  637.0 3.6 collective-permute-done.7
  640.9 0.5 multiply_add_fusion.11
  642.8 0.4 fusion.36
  643.5 0.8 scatter-add.60
  644.4 4.7 collective-permute-start.9
  649.1 3.8 collective-permute-done.8
  653.6 0.5 multiply_add_fusion.7
  655.4 0.4 fusion.25
  656.1 0.8 scatter-add.61
  657.1 4.7 collective-permute-start.11
  661.7 3.0 collective-permute-done.10
  665.2 0.5 multiply_add_fusion.3
  667.0 0.4 fusion.14
  668.1 1.9 sub.150
  (97 shorter events, 11.8 us)
Async XLA Ops:
  0.0 11.8 %copy-start.3 = (s32[1,16384,1]{1,2,0:T(1,128)S(1)}, s32[1,16384,1]{1,2,0:T(1,128)}, u32[]{:S(2)}) copy-start(s32[1,16384,1]{1,2,0:T(1,128)} %param.22) | copy-start | bytes 196612
  57.3 15.4 %copy-start.2 = (f32[3,8,2048]{2,1,0:T(8,128)S(1)}, f32[3,8,2048]{2,1,0:T(8,128)}, u32[]{:S(2)}) copy-start(f32[3,8,2048]{2,1,0:T(8,128)} %param.19) | copy-start | bytes 589828
  57.3 33.0 %copy-start.5 = (s32[3]{0:T(128)S(1)}, s32[3]{0:T(128)}, u32[]{:S(2)}) copy-start(s32[3]{0:T(128)} %constant.202) | copy-start | bytes 40
  57.3 34.2 %copy-start.4 = (s32[3]{0:T(128)S(1)}, s32[3]{0:T(128)}, u32[]{:S(2)}) copy-start(s32[3]{0:T(128)} %constant.205) | copy-start | bytes 40
  64.0 24.9 %all-to-all-start = ((f32[7,8,2560]{2,0,1:T(8,128)}), f32[7,8,2560]{2,0,1:T(8,128)S(1)}, u32[]{:S(2)}, u32[]{:S(2)}) async-start(f32[7,8,2560]{2,0,1:T(8,128)} %copy.35), calls=%async_computation | async-start | bytes 1310720 | tf_op jit(solution)/shard_map/all_to_all | solution.py:104
  71.3 494.9 %collective-permute-start = (f32[1,3,3,8,2048]{4,3,2,1,0:T(8,128)}, f32[1,3,3,8,2048]{4,3,2,1,0:T(8,128)S(1)}, u32[]{:S(2)}, u32[]{:S(2)}) collective-permute-start(f32[1,3,3,8,2048]{4,3,2,1,0:T(8,128)} %param.18), channel_id=1, source_target_pairs={{1,0},{3,2},{5,4},{7,6},{9,8},{11,10},{13,12},{15,14},{17,16},{19,... | collective-permute-start | bytes 1769480 | tf_op jit(solution)/shard_map/ppermute | solution.py:19
  72.7 15.0 %collective-permute-start.4 = (f32[3,1,2048]{2,0,1:T(4,128)S(1)}, f32[3,1,2048]{2,0,1:T(4,128)S(1)}, u32[]{:S(2)}, u32[]{:S(2)}) collective-permute-start(f32[3,1,2048]{2,0,1:T(4,128)S(1)} %copy.48), channel_id=1, source_target_pairs={{0,2},{2,4},{4,6},{6,8},{8,10},{10,12},{12,14},{14,0},{1,3},{3,5},... | collective-permute-start | bytes 73736 | tf_op jit(solution)/shard_map/ppermute | solution.py:34
  74.8 544.3 %collective-permute-start.5 = (f32[3,1,2048]{2,0,1:T(4,128)S(1)}, f32[3,1,2048]{2,0,1:T(4,128)S(1)}, u32[]{:S(2)}, u32[]{:S(2)}) collective-permute-start(f32[3,1,2048]{2,0,1:T(4,128)S(1)} %copy.49), channel_id=1, source_target_pairs={{2,0},{4,2},{6,4},{8,6},{10,8},{12,10},{14,12},{0,14},{3,1},{5,3},... | collective-permute-start | bytes 73736 | tf_op jit(solution)/shard_map/ppermute | solution.py:37
  566.0 7.7 %collective-permute-start.1 = (f32[12,2048]{1,0:T(8,128)S(1)}, f32[12,2048]{1,0:T(8,128)S(1)}, u32[]{:S(2)}, u32[]{:S(2)}) collective-permute-start(f32[12,2048]{1,0:T(8,128)S(1)} %slice_bitcast_fusion), channel_id=1, source_target_pairs={{14,0},{0,2},{2,4},{4,6},{6,8},{8,10},{10,12},{12,14},{15,1},{1,3}... | collective-permute-start | bytes 294920 | tf_op jit(solution)/shard_map/ppermute | solution.py:25
  573.8 1.0 copy-start
  574.9 52.3 %copy-start.1 = (f32[12,8,2048]{2,0,1:T(8,128)S(1)}, f32[12,8,2048]{2,0,1:T(8,128)}, u32[]{:S(2)}) copy-start(f32[12,8,2048]{2,0,1:T(8,128)} %copy-done) | copy-start | bytes 2359300
  575.8 45.8 %collective-permute-start.2 = (f32[9,1,2048]{2,0,1:T(8,128)S(1)}, f32[9,1,2048]{2,0,1:T(8,128)S(1)}, u32[]{:S(2)}, u32[]{:S(2)}) collective-permute-start(f32[9,1,2048]{2,0,1:T(8,128)S(1)} %get-tuple-element.146), channel_id=1, source_target_pairs={{0,2},{2,4},{4,6},{6,8},{8,10},{10,12},{12,14},{14,0},{1,3},{3,5},... | collective-permute-start | bytes 221192 | tf_op jit(solution)/shard_map/ppermute | solution.py:34
  619.0 6.3 collective-permute-start.3
  629.2 7.8 %collective-permute-start.6 = (f32[9,1,2048]{2,0,1:T(8,128)S(1)}, f32[9,1,2048]{2,0,1:T(8,128)S(1)}, u32[]{:S(2)}, u32[]{:S(2)}) collective-permute-start(f32[9,1,2048]{2,0,1:T(8,128)S(1)} %get-tuple-element.144), channel_id=1, source_target_pairs={{0,2},{2,4},{4,6},{6,8},{8,10},{10,12},{12,14},{14,0},{1,3},{3,5},... | collective-permute-start | bytes 221192 | tf_op jit(solution)/shard_map/ppermute | solution.py:34
  632.2 8.3 %collective-permute-start.7 = (f32[9,1,2048]{2,0,1:T(8,128)S(1)}, f32[9,1,2048]{2,0,1:T(8,128)S(1)}, u32[]{:S(2)}, u32[]{:S(2)}) collective-permute-start(f32[9,1,2048]{2,0,1:T(8,128)S(1)} %get-tuple-element.145), channel_id=1, source_target_pairs={{2,0},{4,2},{6,4},{8,6},{10,8},{12,10},{14,12},{0,14},{3,1},{5,3},... | collective-permute-start | bytes 221192 | tf_op jit(solution)/shard_map/ppermute | solution.py:37
  644.4 8.6 %collective-permute-start.8 = (f32[9,1,2048]{2,0,1:T(8,128)S(1)}, f32[9,1,2048]{2,0,1:T(8,128)S(1)}, u32[]{:S(2)}, u32[]{:S(2)}) collective-permute-start(f32[9,1,2048]{2,0,1:T(8,128)S(1)} %get-tuple-element.142), channel_id=1, source_target_pairs={{0,2},{2,4},{4,6},{6,8},{8,10},{10,12},{12,14},{14,0},{1,3},{3,5},... | collective-permute-start | bytes 221192 | tf_op jit(solution)/shard_map/ppermute | solution.py:34
  644.4 8.8 %collective-permute-start.9 = (f32[9,1,2048]{2,0,1:T(8,128)S(1)}, f32[9,1,2048]{2,0,1:T(8,128)S(1)}, u32[]{:S(2)}, u32[]{:S(2)}) collective-permute-start(f32[9,1,2048]{2,0,1:T(8,128)S(1)} %get-tuple-element.143), channel_id=1, source_target_pairs={{2,0},{4,2},{6,4},{8,6},{10,8},{12,10},{14,12},{0,14},{3,1},{5,3},... | collective-permute-start | bytes 221192 | tf_op jit(solution)/shard_map/ppermute | solution.py:37
  656.9 7.8 %collective-permute-start.10 = (f32[9,1,2048]{2,0,1:T(8,128)S(1)}, f32[9,1,2048]{2,0,1:T(8,128)S(1)}, u32[]{:S(2)}, u32[]{:S(2)}) collective-permute-start(f32[9,1,2048]{2,0,1:T(8,128)S(1)} %get-tuple-element.140), channel_id=1, source_target_pairs={{0,2},{2,4},{4,6},{6,8},{8,10},{10,12},{12,14},{14,0},{1,3},{3,5},... | collective-permute-start | bytes 221192 | tf_op jit(solution)/shard_map/ppermute | solution.py:34
  657.1 7.8 %collective-permute-start.11 = (f32[9,1,2048]{2,0,1:T(8,128)S(1)}, f32[9,1,2048]{2,0,1:T(8,128)S(1)}, u32[]{:S(2)}, u32[]{:S(2)}) collective-permute-start(f32[9,1,2048]{2,0,1:T(8,128)S(1)} %get-tuple-element.141), channel_id=1, source_target_pairs={{2,0},{4,2},{6,4},{8,6},{10,8},{12,10},{14,12},{0,14},{3,1},{5,3},... | collective-permute-start | bytes 221192 | tf_op jit(solution)/shard_map/ppermute | solution.py:37
where the time goes:
time: 670 us
  other arithmetic  492 us (73%)
  starting transfers between devices  71.1 us (11%)
  local copies, waits for them, and re-layouts  67.2 us (10%)
  waiting for transfers between devices  38.5 us (6%)
    unnamed x10, other arithmetic  475 us
    ppermute x5, starting transfers between devices, padded(): lax.ppermute(lax.slice_in_dim(block, block.shape[dim] - width, None, axis...  48.6 us
    scatter x1, local copies, waits for them, and re-layouts, body(): jnp.zeros((7, tiles * capacity), jnp.float32).at[:, position]  45.3 us
    ppermute x5, waiting for transfers between devices, padded(): lax.ppermute(lax.slice_in_dim(block, block.shape[dim] - width, None, axis...  22.5 us
    ppermute x5, starting transfers between devices, padded(): lax.ppermute(lax.slice_in_dim(block, 0, width, axis=dim), axis, backward)  13.8 us
  transfers between devices with their start and end apart: 13, of which 11 were waited for; matrix products, arithmetic and copies ran while one was open for 71% of the time, Pallas kernels for 0%

commit v1 on v0

--- a/solution.py
+++ b/solution.py
@@ -1,10 +1,16 @@
+import functools
+
 import jax
 import jax.numpy as jnp
 from jax import lax
+from jax.experimental import pallas as pl
+from jax.experimental.pallas import tpu as pltpu
 from jax.sharding import PartitionSpec as P
 
 STEPS = 4
-
+LANES = 128
+WINDOW = 256
+FIELDS = 6
 
 time_step = 0.4
 friction = 0.05
@@ -12,17 +18,7 @@
 coriolis_slope = 0.2
 coupling = ((1.0, 0.5, 0.25), (0.5, 1.0, 0.5), (0.25, 0.5, 1.0))
 
-
-def shifted(block, axis, distance):
-    devices = range(lax.axis_size(axis))
-    route = [(i - distance, i) for i in devices if i - distance in devices]
-    return lax.ppermute(block, axis, route)
-
-
-def shifted_2(block, axis, distance):
-    devices = range(lax.axis_size(axis))
-    route = [((i - distance) % len(devices), i) for i in devices]
-    return lax.ppermute(block, axis, route)
+NT = (((1,), (1,)), ((), ()))
 
 
 def padded(block, sides, width):
@@ -75,6 +71,232 @@
     return jnp.concatenate([new_height, new_east, new_north], axis=0)
 
 
+def spread(row, rows):
+    part = jnp.broadcast_to(row, (16, row.shape[1])).astype(jnp.bfloat16)
+    return jnp.concatenate([part] * (rows // 16), axis=0)
+
+
+def one_hot(index_row, rows):
+    places = lax.broadcasted_iota(jnp.int32, (rows, index_row.shape[1]), 0)
+    return jnp.where(places == index_row, 1.0, 0.0)
+
+
+def route_kernel(
+    tiles,
+    capacity,
+    columns,
+    tile_rows,
+    width,
+    count_ref,
+    cell_ref,
+    plane_ref,
+    owner_ref,
+    innov_ref,
+    weight_ref,
+    out_ref,
+    key_ref,
+    pos_ref,
+    piece_ref,
+    acc_ref,
+):
+    lines = cell_ref.shape[0]
+    buckets = columns // WINDOW
+    keys = tiles * buckets
+    slot_rows = tiles * capacity // width
+    place = lax.broadcasted_iota(jnp.int32, (lines, LANES), 0) * LANES + lax.broadcasted_iota(
+        jnp.int32, (lines, LANES), 1
+    )
+    live = place < count_ref[0, 0]
+    cell = cell_ref[...]
+    column = jnp.bitwise_and(cell, columns - 1)
+    row = jnp.right_shift(cell, columns.bit_length() - 1)
+    bucket = jnp.right_shift(column, WINDOW.bit_length() - 1)
+    key_ref[...] = jnp.where(live, owner_ref[...] * buckets + bucket, keys)
+    piece_ref[0] = (plane_ref[...] * tile_rows + row + 1).astype(jnp.float32)
+    piece_ref[1] = (bucket * WINDOW).astype(jnp.float32)
+    piece_ref[2] = jnp.bitwise_and(column, WINDOW - 1).astype(jnp.float32)
+    innovation = innov_ref[...]
+    for corner in range(4):
+        value = weight_ref[corner] * innovation
+        high = value.astype(jnp.bfloat16).astype(jnp.float32)
+        piece_ref[3 + 2 * corner] = high
+        piece_ref[4 + 2 * corner] = value - high
+
+    def count_step(line, total):
+        for extra in range(8):
+            total += one_hot(key_ref[pl.ds(line * 8 + extra, 1), :], keys)
+        return total
+
+    total = lax.fori_loop(0, lines // 8, count_step, jnp.zeros((keys, LANES), jnp.float32))
+    mine = lax.broadcasted_iota(jnp.int32, (keys, keys), 0)
+    other = lax.broadcasted_iota(jnp.int32, (keys, keys), 1)
+    shift = buckets.bit_length() - 1
+    same_owner = jnp.right_shift(mine, shift) == jnp.right_shift(other, shift)
+    before = jnp.where(same_owner & (other < mine), 1.0, 0.0).astype(jnp.bfloat16)
+    ahead = jnp.dot(before, total.astype(jnp.bfloat16), preferred_element_type=jnp.float32)
+    owner_of = jnp.right_shift(lax.broadcasted_iota(jnp.int32, (keys, 1), 0), shift)
+    base = jnp.sum(ahead, axis=1, keepdims=True) + (owner_of * capacity).astype(jnp.float32)
+    triangle = jnp.where(
+        lax.broadcasted_iota(jnp.int32, (256, 256), 0)
+        < lax.broadcasted_iota(jnp.int32, (256, 256), 1),
+        1.0,
+        0.0,
+    ).astype(jnp.bfloat16)
+
+    def rank_step(step, base):
+        for extra in range(4):
+            line = step * 8 + extra * 2
+            key = jnp.concatenate(
+                [key_ref[pl.ds(line, 1), :], key_ref[pl.ds(line + 1, 1), :]], axis=1
+            )
+            hits = one_hot(key, keys)
+            earlier = jnp.dot(
+                hits.astype(jnp.bfloat16), triangle, preferred_element_type=jnp.float32
+            )
+            position = jnp.sum(hits * (earlier + base), axis=0, keepdims=True).astype(jnp.int32)
+            position = jnp.where(key < keys, position, -1)
+            pos_ref[pl.ds(line, 1), :] = position[:, :LANES]
+            pos_ref[pl.ds(line + 1, 1), :] = position[:, LANES:]
+            base += jnp.sum(hits, axis=1, keepdims=True)
+        return base
+
+    lax.fori_loop(0, lines // 8, rank_step, base)
+    acc_ref[...] = jnp.zeros_like(acc_ref)
+    log_width = width.bit_length() - 1
+
+    def move_step(step, carry):
+        span = range(8)
+        slots, lefts = [], []
+        for extra in span:
+            position = pos_ref[pl.ds(step * 8 + extra, 1), :]
+            slots.append(one_hot(jnp.right_shift(position, log_width), slot_rows).astype(jnp.bfloat16))
+            lefts.append(one_hot(jnp.bitwise_and(position, width - 1), width).astype(jnp.bfloat16))
+        lane_hits = jnp.concatenate(lefts, axis=1)
+        for piece in range(11):
+            part = jnp.concatenate(
+                [
+                    slots[extra] * spread(piece_ref[piece, pl.ds(step * 8 + extra, 1), :], slot_rows)
+                    for extra in span
+                ],
+                axis=1,
+            )
+            field = 0 if piece == 0 else (piece + 1) // 2
+            acc_ref[field] += lax.dot_general(
+                part, lane_hits, NT, preferred_element_type=jnp.float32
+            )
+        return carry
+
+    lax.fori_loop(0, lines // 8, move_step, 0)
+    per_owner = capacity // width
+    for owner in range(tiles):
+        for field in range(FIELDS):
+            out_ref[owner, field * per_owner : (field + 1) * per_owner, :] = acc_ref[
+                field, owner * per_owner : (owner + 1) * per_owner, :
+            ]
+
+
+def route(cell, plane, owner, innovation, weights, count, tiles, capacity, columns, tile_rows):
+    lines = cell.shape[0]
+    width = 256 if capacity % 256 == 0 else LANES
+    slot_rows = tiles * capacity // width
+    vmem = pl.BlockSpec(memory_space=pltpu.VMEM)
+    return pl.pallas_call(
+        functools.partial(route_kernel, tiles, capacity, columns, tile_rows, width),
+        out_shape=jax.ShapeDtypeStruct((tiles, FIELDS * (capacity // width), width), jnp.float32),
+        in_specs=[pl.BlockSpec(memory_space=pltpu.SMEM)] + [vmem] * 5,
+        out_specs=vmem,
+        scratch_shapes=[
+            pltpu.VMEM((lines, LANES), jnp.int32),
+            pltpu.VMEM((lines, LANES), jnp.int32),
+            pltpu.VMEM((11, lines, LANES), jnp.float32),
+            pltpu.VMEM((FIELDS, slot_rows, width), jnp.float32),
+        ],
+        compiler_params=pltpu.CompilerParams(vmem_limit_bytes=48 * 1024 * 1024),
+        name="route",
+    )(count, cell, plane, owner, innovation, weights)
+
+
+def force_kernel(planes, tile_rows, columns, low_ref, high_ref, in_ref, out_ref, carry_ref, acc_ref):
+    tiles, depth, width = in_ref.shape
+    per_tile = depth // FIELDS
+    cells = planes * tile_rows
+    acc_ref[...] = jnp.zeros_like(acc_ref)
+
+    def source_step(source, carry):
+        def block_step(block, carry):
+            def field(number):
+                return in_ref[source, pl.ds(number * per_tile + block, 1), :]
+
+            line = field(0).astype(jnp.int32) - 1
+            column = field(1).astype(jnp.int32)
+            line_hits = one_hot(line, cells).astype(jnp.bfloat16)
+            highs, lows = [], []
+            for corner in range(4):
+                value = field(2 + corner)
+                high = value.astype(jnp.bfloat16).astype(jnp.float32)
+                highs.append(line_hits * spread(high, cells))
+                lows.append(line_hits * spread(value - high, cells))
+            left = jnp.concatenate(
+                [jnp.concatenate(highs, axis=0), jnp.concatenate(lows, axis=0)], axis=1
+            )
+
+            def window_step(window, carry):
+                hits = one_hot(column - window * WINDOW, WINDOW).astype(jnp.bfloat16)
+                right = jnp.concatenate([hits, hits], axis=1)
+                acc_ref[window] += lax.dot_general(
+                    left, right, NT, preferred_element_type=jnp.float32
+                )
+                return carry
+
+            number = source * per_tile + block
+            lax.fori_loop(low_ref[number], high_ref[number] + 1, window_step, 0)
+            return carry
+
+        return lax.fori_loop(0, per_tile, block_step, carry)
+
+    lax.fori_loop(0, tiles, source_step, 0)
+    row = lax.broadcasted_iota(jnp.int32, (tile_rows, columns), 0)
+    for plane in range(planes):
+
+        def gathered(corner):
+            first = corner * cells + plane * tile_rows
+            return jnp.concatenate(
+                [acc_ref[w, first : first + tile_rows, :] for w in range(columns // WINDOW)],
+                axis=1,
+            )
+
+        here = gathered(0) + pltpu.roll(gathered(1), 1, axis=1)
+        below = gathered(2) + pltpu.roll(gathered(3), 1, axis=1)
+        below = pltpu.roll(below, 1, axis=0)
+        out_ref[plane] = here + jnp.where(row > 0, below, 0.0)
+        carry_ref[plane] = jnp.where(row == 0, below, 0.0)
+
+
+def force(arrived, planes, tile_rows, columns):
+    tiles, depth, width = arrived.shape
+    per_tile = depth // FIELDS
+    line = arrived[:, :per_tile]
+    column = arrived[:, per_tile : 2 * per_tile]
+    low = jnp.min(jnp.where(line > 0, column, float(columns)), axis=2).reshape(tiles * per_tile)
+    high = jnp.max(jnp.where(line > 0, column, -1.0), axis=2).reshape(tiles * per_tile)
+    low = jnp.floor(low / WINDOW).astype(jnp.int32)
+    high = jnp.floor(high / WINDOW).astype(jnp.int32)
+    vmem = pl.BlockSpec(memory_space=pltpu.VMEM)
+    smem = pl.BlockSpec(memory_space=pltpu.SMEM)
+    shape = jax.ShapeDtypeStruct((planes, tile_rows, columns), jnp.float32)
+    return pl.pallas_call(
+        functools.partial(force_kernel, planes, tile_rows, columns),
+        out_shape=(shape, shape),
+        in_specs=[smem, smem, vmem],
+        out_specs=(vmem, vmem),
+        scratch_shapes=[
+            pltpu.VMEM((columns // WINDOW, 4 * planes * tile_rows, WINDOW), jnp.float32)
+        ],
+        compiler_params=pltpu.CompilerParams(vmem_limit_bytes=48 * 1024 * 1024),
+        name="force",
+    )(low, high, arrived)
+
+
 def body(
     adjoint_in, layer_depth, obs_cell, obs_plane, obs_owner, innovation, obs_weight, obs_count
 ):
@@ -85,39 +307,26 @@
     obs_rows = obs_cell.shape[1]
     capacity = 5 * obs_rows // (4 * tiles)
     planes = STEPS * layer_count
-    following = shifted(adjoint_in, "tm", -1)
-    is_live = jnp.arange(obs_rows, dtype=jnp.int32) < obs_count[0, 0]
-    owner_tile = obs_owner[0, :, 0]
-    target = jnp.where(is_live, owner_tile, tiles)
-    owner_hits = (jnp.arange(tiles, dtype=jnp.int32)[:, None] == target[None, :]).astype(jnp.int32)
-    running = jnp.cumsum(owner_hits, axis=1)
-    slot_rank = jnp.where(is_live, jnp.sum(owner_hits * running, axis=0) - 1, 0)
-    position = target * capacity + slot_rank
-    cell_float = obs_cell[0].astype(jnp.float32)
-    plane_float = obs_plane[0].astype(jnp.float32)
-    innov_rows = innovation[0]
-    weights = obs_weight[:, 0, :]
-    fields = jnp.concatenate(
-        [cell_float[None], plane_float[None], innov_rows[None], weights], axis=0
-    )
-    buffer = jnp.zeros((7, tiles * capacity), jnp.float32).at[:, position].set(fields, mode="drop")
-    arrived = lax.all_to_all(
-        buffer.reshape(7, tiles, capacity), "space", split_axis=1, concat_axis=1, tiled=True
-    )
-    arrived = arrived.reshape(7, tiles * capacity)
-    corner_values = arrived[3:7] * arrived[2][None]
-    cell_index = arrived[0].astype(jnp.int32)
-    plane = arrived[1].astype(jnp.int32)
-    grid_row = cell_index // columns
-    column = cell_index % columns
-    next_col = (column + 1) % columns
-    forcing = jnp.zeros((planes, tile_rows + 1, columns), jnp.float32)
-    forcing = forcing.at[plane, grid_row, column].add(corner_values[0])
-    forcing = forcing.at[plane, grid_row, next_col].add(corner_values[1])
-    forcing = forcing.at[plane, grid_row + 1, column].add(corner_values[2])
-    forcing = forcing.at[plane, grid_row + 1, next_col].add(corner_values[3])
-    carried = shifted_2(forcing[:, tile_rows, :], "space", 1)
-    forcing = forcing[:, :tile_rows, :].at[:, 0, :].add(carried)
+    windows = lax.axis_size("tm")
+    following = lax.ppermute(adjoint_in, "tm", [(i + 1, i) for i in range(windows - 1)])
+    lines = obs_rows // LANES
+    buffer = route(
+        obs_cell.reshape(lines, LANES),
+        obs_plane.reshape(lines, LANES),
+        obs_owner.reshape(lines, LANES),
+        innovation.reshape(lines, LANES),
+        obs_weight.reshape(4, lines, LANES),
+        obs_count,
+        tiles,
+        capacity,
+        columns,
+        tile_rows,
+    )
+    arrived = lax.all_to_all(buffer, "space", split_axis=0, concat_axis=0, tiled=True)
+    forcing, spill = force(arrived, planes, tile_rows, columns)
+    count = lax.axis_size("space")
+    carried = lax.ppermute(spill[:, 0], "space", [(i, (i + 1) % count) for i in range(count)])
+    forcing = forcing.at[:, 0, :].add(carried)
     coriolis = coriolis_mid + coriolis_slope * (
         jnp.arange(columns, dtype=jnp.float32) / columns - 0.5
     )

time: 670 us -> 145 us (0.22)
  other arithmetic: 492 us -> 4.21 us
  Pallas kernels: 0 us -> 68.5 us
  local copies, waits for them, and re-layouts: 67.2 us -> 7.37 us
  starting transfers between devices: 71.1 us -> 40 us
  waiting for transfers between devices: 38.5 us -> 22.4 us
    unnamed x10 -> x0, other arithmetic: 475 us -> none
    pallas_call x0 -> x2, Pallas kernels: none -> 68.5 us  [the longest x1 35.3 us: route(): pl.pallas_call(functools.partial(route_kernel, tiles, capacity, columns,...]
    ppermute x5, starting transfers between devices: 48.6 us -> 1.05 us  [padded(): lax.ppermute(lax.slice_in_dim(block, block.shape[dim] - width, None, axis...]
    scatter x1 -> x0, local copies, waits for them, and re-layouts: 45.3 us -> none  [body(): jnp.zeros((7, tiles * capacity), jnp.float32).at[:, position]]
    ppermute x5, waiting for transfers between devices: 22.5 us -> 9.21 us  [padded(): lax.ppermute(lax.slice_in_dim(block, block.shape[dim] - width, None, axis...]
    all_to_all x1, waiting for transfers between devices: 1.26 us -> 13.2 us  [body(): lax.all_to_all(buffer, 'space', split_axis=0, concat_axis=0, tiled=True)]
    ppermute x5, starting transfers between devices: 13.8 us -> 23.1 us  [padded(): lax.ppermute(lax.slice_in_dim(block, 0, width, axis=dim), axis, backward)]
    ppermute x5, waiting for transfers between devices: 7.79 us -> 0.01 us  [padded(): lax.ppermute(lax.slice_in_dim(block, 0, width, axis=dim), axis, backward)]
  transfers between devices with their start and end apart: 13 -> 13, of which waited for: 11 -> 5; matrix products, arithmetic and copies ran while one was open for 71% -> 1% of each run, Pallas kernels for 0% -> 23%
where the time goes in v1:
time: 145 us; the launch traced here: 144 us
  Pallas kernels  68.5 us (47%)
  starting transfers between devices  40 us (28%)
  waiting for transfers between devices  22.4 us (15%)
  local copies, waits for them, and re-layouts  7.37 us (5%)
  other arithmetic  4.21 us (3%)
    pallas_call x1, Pallas kernels, route(): pl.pallas_call(functools.partial(route_kernel, tiles, capacity, columns,...  35.3 us
    pallas_call x1, Pallas kernels, force(): pl.pallas_call(functools.partial(force_kernel, planes, tile_rows, columns...  33.2 us
    ppermute x5, starting transfers between devices, padded(): lax.ppermute(lax.slice_in_dim(block, 0, width, axis=dim), axis, backward)  23.1 us
    all_to_all x1, waiting for transfers between devices, body(): lax.all_to_all(buffer, 'space', split_axis=0, concat_axis=0, tiled=True)  13.2 us
    ppermute x5, waiting for transfers between devices, padded(): lax.ppermute(lax.slice_in_dim(block, block.shape[dim] - width, None, axis...  9.21 us
    all_to_all x1, starting transfers between devices, body(): lax.all_to_all(buffer, 'space', split_axis=0, concat_axis=0, tiled=True)  7.42 us
    ppermute x1, starting transfers between devices, body(): lax.ppermute(spill[:, 0], 'space', [(i, (i + 1) % count) for i in range(c...  7.09 us
    unnamed x16, local copies, waits for them, and re-layouts  4.38 us
  transfers between devices with their start and end apart: 13, of which 5 were waited for; matrix products, arithmetic and copies ran while one was open for 1% of the time, Pallas kernels for 23%

profile of v1, /device:TPU:0, one launch (start us, length us, event | category | flops | bytes accessed | tf_op | source)
XLA Modules:
  0.0 143.6 jit_solution(9010545518138824010)
XLA Ops:
  0.7 0.9 copy-done
  1.6 0.8 copy-done.1
  2.4 0.8 copy-done.2
  3.3 0.8 copy-done.3
  4.1 0.8 copy-done.4
  5.0 35.3 %route.1 = f32[8,60,256]{2,1,0:T(8,128)} custom-call(s32[1,1]{1,0:T(1,128)S(6)} %copy.19.count_ref, s32[128,128]{1,0:T(8,128)S(1)} %bitcast.21, s32[128,128]{1,0:T(8,128)S(1)} %bitcast.22, s32[128,128]{1,0:T(8,128)S(1)} %bitcast.23, f32[128,128]{1,0:T(8,128)S(1)} %bitcast.24, f32[4,128,128]{2,1,0:T(8,128)S(1)} %bitcast.20), custom_call_target="tpu_custom_call" | custom-call | tf_op jit(solution)/shard_map/route/pallas_call | solution.py:203
  40.3 7.4 %all-to-all-start = ((f32[8,60,256]{2,1,0:T(8,128)}), f32[8,60,256]{2,1,0:T(8,128)S(1)}, u32[]{:S(2)}, u32[]{:S(2)}) async-start(f32[8,60,256]{2,1,0:T(8,128)} %route.1), calls=%async_computation | async-start | bytes 1048576 | tf_op jit(solution)/shard_map/all_to_all | solution.py:325
  47.7 1.3 collective-permute-start
  49.0 13.2 %all-to-all-done.in_ref = f32[8,60,256]{2,1,0:T(8,128)S(1)} async-done(((f32[8,60,256]{2,1,0:T(8,128)}), f32[8,60,256]{2,1,0:T(8,128)S(1)}, u32[]{:S(2)}, u32[]{:S(2)}) %all-to-all-start) | async-done | bytes 491552 | tf_op jit(solution)/shard_map/all_to_all | solution.py:325
  62.5 33.2 %force.1 = (f32[12,8,2048]{2,1,0:T(8,128)S(1)}, f32[12,8,2048]{2,1,0:T(8,128)S(1)}) custom-call(s32[80]{0:T(128)S(1)} %convert_element_type.11.low_ref, s32[80]{0:T(128)S(1)} %convert_element_type.13.high_ref, f32[8,60,256]{2,1,0:T(8,128)S(1)} %all-to-all-done.in_ref), custom_call_target="tpu_custom_call" | custom-call | tf_op jit(solution)/shard_map/force/pallas_call | solution.py:287
  95.8 7.1 %collective-permute-start.1 = (f32[12,2048]{1,0:T(8,128)S(1)}, f32[12,2048]{1,0:T(8,128)S(1)}, u32[]{:S(2)}, u32[]{:S(2)}) collective-permute-start(f32[12,2048]{1,0:T(8,128)S(1)} %bitcast.27), channel_id=1, source_target_pairs={{0,2},{2,4},{4,6},{6,8},{8,10},{10,12},{12,14},{14,0},{1,3},{3,5},... | collective-permute-start | bytes 294920 | tf_op jit(solution)/shard_map/ppermute | solution.py:328
  102.9 0.8 collective-permute-start.4
  103.8 4.0 %collective-permute-start.5 = (f32[3,1,2048]{2,1,0:T(1,128)S(1)}, f32[3,1,2048]{2,1,0:T(1,128)S(1)}, u32[]{:S(2)}, u32[]{:S(2)}) collective-permute-start(f32[3,1,2048]{2,1,0:T(1,128)S(1)} %get-tuple-element.176), channel_id=1, source_target_pairs={{2,0},{4,2},{6,4},{8,6},{10,8},{12,10},{14,12},{0,14},{3,1},{5,3},... | collective-permute-start | bytes 73736 | tf_op jit(solution)/shard_map/ppermute | solution.py:33
  107.8 0.5 copy.9
  108.4 0.6 scatter-add.16
  109.1 4.7 %collective-permute-start.3 = (f32[9,1,2048]{2,1,0:T(1,128)S(1)}, f32[9,1,2048]{2,1,0:T(1,128)S(1)}, u32[]{:S(2)}, u32[]{:S(2)}) collective-permute-start(f32[9,1,2048]{2,1,0:T(1,128)S(1)} %get-tuple-element.134), channel_id=1, source_target_pairs={{2,0},{4,2},{6,4},{8,6},{10,8},{12,10},{14,12},{0,14},{3,1},{5,3},... | collective-permute-start | bytes 221192 | tf_op jit(solution)/shard_map/ppermute | solution.py:33
  113.9 2.3 %collective-permute-done.2 = f32[9,1,2048]{2,1,0:T(1,128)S(1)} collective-permute-done((f32[9,1,2048]{2,1,0:T(1,128)S(1)}, f32[9,1,2048]{2,1,0:T(1,128)S(1)}, u32[]{:S(2)}, u32[]{:S(2)}) %collective-permute-start.2) | collective-permute-done | bytes 73760 | tf_op jit(solution)/shard_map/ppermute | solution.py:30
  116.2 0.1 fusion.3
  116.4 0.1 fusion.87
  116.5 0.2 multiply_add_fusion.15
  116.8 0.1 fusion.85
  117.0 0.1 fusion.41
  117.2 0.1 fusion.46
  117.5 4.8 %collective-permute-start.7 = (f32[9,1,2048]{2,1,0:T(1,128)S(1)}, f32[9,1,2048]{2,1,0:T(1,128)S(1)}, u32[]{:S(2)}, u32[]{:S(2)}) collective-permute-start(f32[9,1,2048]{2,1,0:T(1,128)S(1)} %get-tuple-element.132), channel_id=1, source_target_pairs={{2,0},{4,2},{6,4},{8,6},{10,8},{12,10},{14,12},{0,14},{3,1},{5,3},... | collective-permute-start | bytes 221192 | tf_op jit(solution)/shard_map/ppermute | solution.py:33
  122.3 2.3 %collective-permute-done.6 = f32[9,1,2048]{2,1,0:T(1,128)S(1)} collective-permute-done((f32[9,1,2048]{2,1,0:T(1,128)S(1)}, f32[9,1,2048]{2,1,0:T(1,128)S(1)}, u32[]{:S(2)}, u32[]{:S(2)}) %collective-permute-start.6) | collective-permute-done | bytes 73760 | tf_op jit(solution)/shard_map/ppermute | solution.py:30
  124.6 0.1 fusion.2
  124.8 0.1 fusion.84
  124.9 0.2 multiply_add_fusion.11
  125.2 0.1 fusion.82
  125.4 0.1 fusion.35
  125.5 0.1 fusion.30
  125.9 4.8 %collective-permute-start.9 = (f32[9,1,2048]{2,1,0:T(1,128)S(1)}, f32[9,1,2048]{2,1,0:T(1,128)S(1)}, u32[]{:S(2)}, u32[]{:S(2)}) collective-permute-start(f32[9,1,2048]{2,1,0:T(1,128)S(1)} %get-tuple-element.130), channel_id=1, source_target_pairs={{2,0},{4,2},{6,4},{8,6},{10,8},{12,10},{14,12},{0,14},{3,1},{5,3},... | collective-permute-start | bytes 221192 | tf_op jit(solution)/shard_map/ppermute | solution.py:33
  130.8 2.4 %collective-permute-done.8 = f32[9,1,2048]{2,1,0:T(1,128)S(1)} collective-permute-done((f32[9,1,2048]{2,1,0:T(1,128)S(1)}, f32[9,1,2048]{2,1,0:T(1,128)S(1)}, u32[]{:S(2)}, u32[]{:S(2)}) %collective-permute-start.8) | collective-permute-done | bytes 73760 | tf_op jit(solution)/shard_map/ppermute | solution.py:30
  133.2 0.1 fusion.1
  133.4 0.1 fusion.81
  133.5 0.2 multiply_add_fusion.7
  133.8 0.1 fusion.79
  134.0 0.1 fusion.24
  134.1 0.1 fusion.19
  134.5 4.8 %collective-permute-start.11 = (f32[9,1,2048]{2,1,0:T(1,128)S(1)}, f32[9,1,2048]{2,1,0:T(1,128)S(1)}, u32[]{:S(2)}, u32[]{:S(2)}) collective-permute-start(f32[9,1,2048]{2,1,0:T(1,128)S(1)} %get-tuple-element.128), channel_id=1, source_target_pairs={{2,0},{4,2},{6,4},{8,6},{10,8},{12,10},{14,12},{0,14},{3,1},{5,3},... | collective-permute-start | bytes 221192 | tf_op jit(solution)/shard_map/ppermute | solution.py:33
  139.3 2.3 %collective-permute-done.10 = f32[9,1,2048]{2,1,0:T(1,128)S(1)} collective-permute-done((f32[9,1,2048]{2,1,0:T(1,128)S(1)}, f32[9,1,2048]{2,1,0:T(1,128)S(1)}, u32[]{:S(2)}, u32[]{:S(2)}) %collective-permute-start.10) | collective-permute-done | bytes 73760 | tf_op jit(solution)/shard_map/ppermute | solution.py:30
  141.6 0.1 fusion
  141.8 0.1 fusion.78
  142.0 0.2 multiply_add_fusion.3
  142.2 0.1 fusion.76
  142.4 0.1 fusion.13
  142.6 0.1 fusion.8
  142.8 0.9 sub.135
  (64 shorter events, 2.3 us)
Async XLA Ops:
  0.7 1.0 copy-start
  1.6 0.8 copy-start.1
  2.4 0.8 copy-start.2
  3.3 0.8 copy-start.3
  4.1 0.8 copy-start.4
  40.3 7.4 %copy-start.6 = (f32[1,3,3,8,2048]{4,3,2,1,0:T(8,128)S(1)}, f32[1,3,3,8,2048]{4,3,2,1,0:T(8,128)}, u32[]{:S(2)}) copy-start(f32[1,3,3,8,2048]{4,3,2,1,0:T(8,128)} %param.18) | copy-start | bytes 1769476
  40.3 21.9 %all-to-all-start = ((f32[8,60,256]{2,1,0:T(8,128)}), f32[8,60,256]{2,1,0:T(8,128)S(1)}, u32[]{:S(2)}, u32[]{:S(2)}) async-start(f32[8,60,256]{2,1,0:T(8,128)} %route.1), calls=%async_computation | async-start | bytes 1048576 | tf_op jit(solution)/shard_map/all_to_all | solution.py:325
  47.7 60.0 %collective-permute-start = (f32[1,3,3,8,2048]{4,3,2,1,0:T(8,128)S(1)}, f32[1,3,3,8,2048]{4,3,2,1,0:T(8,128)S(1)}, u32[]{:S(2)}, u32[]{:S(2)}) collective-permute-start(f32[1,3,3,8,2048]{4,3,2,1,0:T(8,128)S(1)} %copy-done.6), channel_id=1, source_target_pairs={{1,0},{3,2},{5,4},{7,6},{9,8},{11,10},{13,12},{15,14},{17,16},{19,... | collective-permute-start | bytes 1769480 | tf_op jit(solution)/shard_map/ppermute | solution.py:311
  95.7 7.2 %copy-start.5 = (f32[3,8,2048]{2,1,0:T(8,128)S(1)}, f32[3,8,2048]{2,1,0:T(8,128)}, u32[]{:S(2)}) copy-start(f32[3,8,2048]{2,1,0:T(8,128)} %param.19) | copy-start | bytes 589828
  95.8 12.4 %collective-permute-start.1 = (f32[12,2048]{1,0:T(8,128)S(1)}, f32[12,2048]{1,0:T(8,128)S(1)}, u32[]{:S(2)}, u32[]{:S(2)}) collective-permute-start(f32[12,2048]{1,0:T(8,128)S(1)} %bitcast.27), channel_id=1, source_target_pairs={{0,2},{2,4},{4,6},{6,8},{8,10},{10,12},{12,14},{14,0},{1,3},{3,5},... | collective-permute-start | bytes 294920 | tf_op jit(solution)/shard_map/ppermute | solution.py:328
  102.9 10.9 %collective-permute-start.4 = (f32[3,1,2048]{2,1,0:T(1,128)S(1)}, f32[3,1,2048]{2,1,0:T(1,128)S(1)}, u32[]{:S(2)}, u32[]{:S(2)}) collective-permute-start(f32[3,1,2048]{2,1,0:T(1,128)S(1)} %get-tuple-element.175), channel_id=1, source_target_pairs={{0,2},{2,4},{4,6},{6,8},{8,10},{10,12},{12,14},{14,0},{1,3},{3,5},... | collective-permute-start | bytes 73736 | tf_op jit(solution)/shard_map/ppermute | solution.py:30
  103.8 10.1 %collective-permute-start.5 = (f32[3,1,2048]{2,1,0:T(1,128)S(1)}, f32[3,1,2048]{2,1,0:T(1,128)S(1)}, u32[]{:S(2)}, u32[]{:S(2)}) collective-permute-start(f32[3,1,2048]{2,1,0:T(1,128)S(1)} %get-tuple-element.176), channel_id=1, source_target_pairs={{2,0},{4,2},{6,4},{8,6},{10,8},{12,10},{14,12},{0,14},{3,1},{5,3},... | collective-permute-start | bytes 73736 | tf_op jit(solution)/shard_map/ppermute | solution.py:33
  109.1 7.1 %collective-permute-start.2 = (f32[9,1,2048]{2,1,0:T(1,128)S(1)}, f32[9,1,2048]{2,1,0:T(1,128)S(1)}, u32[]{:S(2)}, u32[]{:S(2)}) collective-permute-start(f32[9,1,2048]{2,1,0:T(1,128)S(1)} %get-tuple-element.133), channel_id=1, source_target_pairs={{0,2},{2,4},{4,6},{6,8},{8,10},{10,12},{12,14},{14,0},{1,3},{3,5},... | collective-permute-start | bytes 221192 | tf_op jit(solution)/shard_map/ppermute | solution.py:30
  109.1 7.0 %collective-permute-start.3 = (f32[9,1,2048]{2,1,0:T(1,128)S(1)}, f32[9,1,2048]{2,1,0:T(1,128)S(1)}, u32[]{:S(2)}, u32[]{:S(2)}) collective-permute-start(f32[9,1,2048]{2,1,0:T(1,128)S(1)} %get-tuple-element.134), channel_id=1, source_target_pairs={{2,0},{4,2},{6,4},{8,6},{10,8},{12,10},{14,12},{0,14},{3,1},{5,3},... | collective-permute-start | bytes 221192 | tf_op jit(solution)/shard_map/ppermute | solution.py:33
  117.5 7.1 %collective-permute-start.6 = (f32[9,1,2048]{2,1,0:T(1,128)S(1)}, f32[9,1,2048]{2,1,0:T(1,128)S(1)}, u32[]{:S(2)}, u32[]{:S(2)}) collective-permute-start(f32[9,1,2048]{2,1,0:T(1,128)S(1)} %get-tuple-element.131), channel_id=1, source_target_pairs={{0,2},{2,4},{4,6},{6,8},{8,10},{10,12},{12,14},{14,0},{1,3},{3,5},... | collective-permute-start | bytes 221192 | tf_op jit(solution)/shard_map/ppermute | solution.py:30
  117.5 7.0 %collective-permute-start.7 = (f32[9,1,2048]{2,1,0:T(1,128)S(1)}, f32[9,1,2048]{2,1,0:T(1,128)S(1)}, u32[]{:S(2)}, u32[]{:S(2)}) collective-permute-start(f32[9,1,2048]{2,1,0:T(1,128)S(1)} %get-tuple-element.132), channel_id=1, source_target_pairs={{2,0},{4,2},{6,4},{8,6},{10,8},{12,10},{14,12},{0,14},{3,1},{5,3},... | collective-permute-start | bytes 221192 | tf_op jit(solution)/shard_map/ppermute | solution.py:33
  125.9 7.3 %collective-permute-start.8 = (f32[9,1,2048]{2,1,0:T(1,128)S(1)}, f32[9,1,2048]{2,1,0:T(1,128)S(1)}, u32[]{:S(2)}, u32[]{:S(2)}) collective-permute-start(f32[9,1,2048]{2,1,0:T(1,128)S(1)} %get-tuple-element.129), channel_id=1, source_target_pairs={{0,2},{2,4},{4,6},{6,8},{8,10},{10,12},{12,14},{14,0},{1,3},{3,5},... | collective-permute-start | bytes 221192 | tf_op jit(solution)/shard_map/ppermute | solution.py:30
  125.9 7.2 %collective-permute-start.9 = (f32[9,1,2048]{2,1,0:T(1,128)S(1)}, f32[9,1,2048]{2,1,0:T(1,128)S(1)}, u32[]{:S(2)}, u32[]{:S(2)}) collective-permute-start(f32[9,1,2048]{2,1,0:T(1,128)S(1)} %get-tuple-element.130), channel_id=1, source_target_pairs={{2,0},{4,2},{6,4},{8,6},{10,8},{12,10},{14,12},{0,14},{3,1},{5,3},... | collective-permute-start | bytes 221192 | tf_op jit(solution)/shard_map/ppermute | solution.py:33
  134.4 7.2 %collective-permute-start.10 = (f32[9,1,2048]{2,1,0:T(1,128)S(1)}, f32[9,1,2048]{2,1,0:T(1,128)S(1)}, u32[]{:S(2)}, u32[]{:S(2)}) collective-permute-start(f32[9,1,2048]{2,1,0:T(1,128)S(1)} %get-tuple-element.127), channel_id=1, source_target_pairs={{0,2},{2,4},{4,6},{6,8},{8,10},{10,12},{12,14},{14,0},{1,3},{3,5},... | collective-permute-start | bytes 221192 | tf_op jit(solution)/shard_map/ppermute | solution.py:30
  134.5 7.1 %collective-permute-start.11 = (f32[9,1,2048]{2,1,0:T(1,128)S(1)}, f32[9,1,2048]{2,1,0:T(1,128)S(1)}, u32[]{:S(2)}, u32[]{:S(2)}) collective-permute-start(f32[9,1,2048]{2,1,0:T(1,128)S(1)} %get-tuple-element.128), channel_id=1, source_target_pairs={{2,0},{4,2},{6,4},{8,6},{10,8},{12,10},{14,12},{0,14},{3,1},{5,3},... | collective-permute-start | bytes 221192 | tf_op jit(solution)/shard_map/ppermute | solution.py:33

commit v2 on v1

--- a/solution.py
+++ b/solution.py
@@ -11,6 +11,7 @@
 LANES = 128
 WINDOW = 256
 FIELDS = 6
+GROUP = 4
 
 time_step = 0.4
 friction = 0.05
@@ -19,56 +20,6 @@
 coupling = ((1.0, 0.5, 0.25), (0.5, 1.0, 0.5), (0.25, 0.5, 1.0))
 
 NT = (((1,), (1,)), ((), ()))
-
-
-def padded(block, sides, width):
-    for axis, dim in sides:
-        count = lax.axis_size(axis)
-        forward = [(i, i + 1) for i in range(count - 1)]
-        forward.append((count - 1, 0))
-        backward = [(target, source) for source, target in forward]
-        low = lax.ppermute(
-            lax.slice_in_dim(block, block.shape[dim] - width, None, axis=dim), axis, forward
-        )
-        high = lax.ppermute(lax.slice_in_dim(block, 0, width, axis=dim), axis, backward)
-        block = jnp.concatenate([low, block, high], axis=dim)
-    return block
-
-
-def couple_layers(field):
-    return jnp.stack(
-        [
-            coupling[0][m] * field[0] + coupling[1][m] * field[1] + coupling[2][m] * field[2]
-            for m in range(3)
-        ]
-    )
-
-
-def along_rows(field):
-    return (field[:, 2:] - field[:, :-2]) * 0.5
-
-
-def along_cols(field):
-    interior = field[:, 1:-1]
-    return (jnp.roll(interior, -1, axis=2) - jnp.roll(interior, 1, axis=2)) * 0.5
-
-
-def advance(extended, depth_ext, coriolis, layer_count):
-    height = extended[0:layer_count]
-    east = extended[layer_count : 2 * layer_count]
-    north = extended[2 * layer_count : 3 * layer_count]
-    thick = depth_ext * height
-    east_mix = couple_layers(east)
-    north_mix = couple_layers(north)
-    height_in = height[:, 1:-1]
-    east_in = east[:, 1:-1]
-    north_in = north[:, 1:-1]
-    new_height = height_in + time_step * (along_rows(east_mix) + along_cols(north_mix))
-    new_east = east_in + time_step * (along_rows(thick) - coriolis * north_in - friction * east_in)
-    new_north = north_in + time_step * (
-        along_cols(thick) + coriolis * east_in - friction * north_in
-    )
-    return jnp.concatenate([new_height, new_east, new_north], axis=0)
 
 
 def spread(row, rows):
@@ -172,27 +123,29 @@
             slots.append(one_hot(jnp.right_shift(position, log_width), slot_rows).astype(jnp.bfloat16))
             lefts.append(one_hot(jnp.bitwise_and(position, width - 1), width).astype(jnp.bfloat16))
         lane_hits = jnp.concatenate(lefts, axis=1)
-        for piece in range(11):
-            part = jnp.concatenate(
-                [
-                    slots[extra] * spread(piece_ref[piece, pl.ds(step * 8 + extra, 1), :], slot_rows)
-                    for extra in span
-                ],
-                axis=1,
-            )
-            field = 0 if piece == 0 else (piece + 1) // 2
-            acc_ref[field] += lax.dot_general(
-                part, lane_hits, NT, preferred_element_type=jnp.float32
-            )
+        parts = []
+        for extra in span:
+            pieces = [
+                slots[extra] * spread(piece_ref[piece, pl.ds(step * 8 + extra, 1), :], slot_rows)
+                for piece in range(11)
+            ]
+            parts.append(jnp.concatenate(pieces, axis=0))
+        acc_ref[...] += lax.dot_general(
+            jnp.concatenate(parts, axis=1), lane_hits, NT, preferred_element_type=jnp.float32
+        )
         return carry
 
     lax.fori_loop(0, lines // 8, move_step, 0)
     per_owner = capacity // width
     for owner in range(tiles):
         for field in range(FIELDS):
-            out_ref[owner, field * per_owner : (field + 1) * per_owner, :] = acc_ref[
-                field, owner * per_owner : (owner + 1) * per_owner, :
-            ]
+
+            def piece_rows(piece):
+                first = piece * slot_rows + owner * per_owner
+                return acc_ref[first : first + per_owner, :]
+
+            value = piece_rows(0) if field == 0 else piece_rows(2 * field - 1) + piece_rows(2 * field)
+            out_ref[owner, field * per_owner : (field + 1) * per_owner, :] = value
 
 
 def route(cell, plane, owner, innovation, weights, count, tiles, capacity, columns, tile_rows):
@@ -209,52 +162,73 @@
             pltpu.VMEM((lines, LANES), jnp.int32),
             pltpu.VMEM((lines, LANES), jnp.int32),
             pltpu.VMEM((11, lines, LANES), jnp.float32),
-            pltpu.VMEM((FIELDS, slot_rows, width), jnp.float32),
+            pltpu.VMEM((11 * slot_rows, width), jnp.float32),
         ],
         compiler_params=pltpu.CompilerParams(vmem_limit_bytes=48 * 1024 * 1024),
         name="route",
     )(count, cell, plane, owner, innovation, weights)
 
 
-def force_kernel(planes, tile_rows, columns, low_ref, high_ref, in_ref, out_ref, carry_ref, acc_ref):
+def force_kernel(
+    planes, tile_rows, columns, low_ref, high_ref, in_ref, out_ref, spill_ref, acc_ref, item_ref
+):
     tiles, depth, width = in_ref.shape
     per_tile = depth // FIELDS
     cells = planes * tile_rows
+    windows = columns // WINDOW
     acc_ref[...] = jnp.zeros_like(acc_ref)
 
-    def source_step(source, carry):
-        def block_step(block, carry):
-            def field(number):
-                return in_ref[source, pl.ds(number * per_tile + block, 1), :]
-
-            line = field(0).astype(jnp.int32) - 1
-            column = field(1).astype(jnp.int32)
-            line_hits = one_hot(line, cells).astype(jnp.bfloat16)
-            highs, lows = [], []
-            for corner in range(4):
-                value = field(2 + corner)
-                high = value.astype(jnp.bfloat16).astype(jnp.float32)
-                highs.append(line_hits * spread(high, cells))
-                lows.append(line_hits * spread(value - high, cells))
-            left = jnp.concatenate(
-                [jnp.concatenate(highs, axis=0), jnp.concatenate(lows, axis=0)], axis=1
-            )
-
-            def window_step(window, carry):
-                hits = one_hot(column - window * WINDOW, WINDOW).astype(jnp.bfloat16)
-                right = jnp.concatenate([hits, hits], axis=1)
-                acc_ref[window] += lax.dot_general(
-                    left, right, NT, preferred_element_type=jnp.float32
-                )
-                return carry
-
+    def list_source(source, count):
+        def list_block(block, count):
             number = source * per_tile + block
-            lax.fori_loop(low_ref[number], high_ref[number] + 1, window_step, 0)
-            return carry
-
-        return lax.fori_loop(0, per_tile, block_step, carry)
-
-    lax.fori_loop(0, tiles, source_step, 0)
+
+            def list_window(window, count):
+                item_ref[0, count] = source
+                item_ref[1, count] = block
+                item_ref[2, count] = window
+                item_ref[3, count] = window
+                return count + 1
+
+            return lax.fori_loop(low_ref[number], high_ref[number] + 1, list_window, count)
+
+        return lax.fori_loop(0, per_tile, list_block, count)
+
+    count = lax.fori_loop(0, tiles, list_source, 0)
+    for extra in range(GROUP):
+        item_ref[0, count + extra] = 0
+        item_ref[1, count + extra] = 0
+        item_ref[2, count + extra] = windows
+        item_ref[3, count + extra] = 0
+
+    def product(item):
+        source, block = item_ref[0, item], item_ref[1, item]
+
+        def field(number):
+            return in_ref[source, pl.ds(number * per_tile + block, 1), :]
+
+        line = field(0).astype(jnp.int32) - 1
+        column = field(1).astype(jnp.int32)
+        line_hits = one_hot(line, cells).astype(jnp.bfloat16)
+        highs, lows = [], []
+        for corner in range(4):
+            value = field(2 + corner)
+            high = value.astype(jnp.bfloat16).astype(jnp.float32)
+            highs.append(line_hits * spread(high, cells))
+            lows.append(line_hits * spread(value - high, cells))
+        left = jnp.concatenate(
+            [jnp.concatenate(highs, axis=0), jnp.concatenate(lows, axis=0)], axis=1
+        )
+        hits = one_hot(column - item_ref[2, item] * WINDOW, WINDOW).astype(jnp.bfloat16)
+        right = jnp.concatenate([hits, hits], axis=1)
+        return lax.dot_general(left, right, NT, preferred_element_type=jnp.float32)
+
+    def group_step(group, carry):
+        found = [product(group * GROUP + extra) for extra in range(GROUP)]
+        for extra in range(GROUP):
+            acc_ref[item_ref[3, group * GROUP + extra]] += found[extra]
+        return carry
+
+    lax.fori_loop(0, (count + GROUP - 1) // GROUP, group_step, 0)
     row = lax.broadcasted_iota(jnp.int32, (tile_rows, columns), 0)
     for plane in range(planes):
 
@@ -269,7 +243,7 @@
         below = gathered(2) + pltpu.roll(gathered(3), 1, axis=1)
         below = pltpu.roll(below, 1, axis=0)
         out_ref[plane] = here + jnp.where(row > 0, below, 0.0)
-        carry_ref[plane] = jnp.where(row == 0, below, 0.0)
+        spill_ref[plane : plane + 1, :] = below[0:1, :]
 
 
 def force(arrived, planes, tile_rows, columns):
@@ -286,15 +260,166 @@
     shape = jax.ShapeDtypeStruct((planes, tile_rows, columns), jnp.float32)
     return pl.pallas_call(
         functools.partial(force_kernel, planes, tile_rows, columns),
-        out_shape=(shape, shape),
+        out_shape=(shape, jax.ShapeDtypeStruct((planes, columns), jnp.float32)),
         in_specs=[smem, smem, vmem],
         out_specs=(vmem, vmem),
         scratch_shapes=[
-            pltpu.VMEM((columns // WINDOW, 4 * planes * tile_rows, WINDOW), jnp.float32)
+            pltpu.VMEM((columns // WINDOW, 4 * planes * tile_rows, WINDOW), jnp.float32),
+            pltpu.SMEM((4, tiles * (per_tile * 2 + 2 * columns // WINDOW) + GROUP), jnp.int32),
         ],
         compiler_params=pltpu.CompilerParams(vmem_limit_bytes=48 * 1024 * 1024),
         name="force",
     )(low, high, arrived)
+
+
+def stencil_kernel(
+    adjoint_ref,
+    depth_ref,
+    forcing_ref,
+    spill_ref,
+    out_ref,
+    edge_out,
+    edge_in,
+    depth_out,
+    depth_in,
+    spill_in,
+    send_sem,
+    recv_sem,
+):
+    layers, tile_rows, columns = depth_ref.shape
+    tiles = lax.axis_size("space")
+    me = lax.axis_index("space")
+    after = lax.rem(me + 1, tiles)
+    before = lax.rem(me + tiles - 1, tiles)
+    barrier = pltpu.get_barrier_semaphore()
+    for neighbour in (before, after):
+        pl.semaphore_signal(
+            barrier,
+            inc=1,
+            device_id={"space": neighbour},
+            device_id_type=pl.DeviceIdType.MESH,
+        )
+    pl.semaphore_wait(barrier, 2)
+
+    def copy(source, target, number, neighbour):
+        return pltpu.make_async_remote_copy(
+            src_ref=source,
+            dst_ref=target,
+            send_sem=send_sem.at[number],
+            recv_sem=recv_sem.at[number],
+            device_id={"space": neighbour},
+            device_id_type=pl.DeviceIdType.MESH,
+        )
+
+    spill_copy = copy(spill_ref, spill_in, 2 * STEPS, after)
+    depth_copy = copy(depth_out, depth_in, 2 * STEPS + 1, before)
+    spill_copy.start()
+    for layer in range(layers):
+        depth_out[layer : layer + 1, :] = depth_ref[layer, 0:1, :]
+    depth_copy.start()
+
+    row = lax.broadcasted_iota(jnp.int32, (tile_rows, columns), 0)
+    first, last = row == 0, row == tile_rows - 1
+    place = lax.broadcasted_iota(jnp.int32, (tile_rows, columns), 1).astype(jnp.float32)
+    coriolis = coriolis_mid + coriolis_slope * (place / columns - 0.5)
+    half = 0.5 * time_step
+
+    def rows_inside(field):
+        ahead = jnp.where(last, 0.0, pltpu.roll(field, tile_rows - 1, axis=0))
+        behind = jnp.where(first, 0.0, pltpu.roll(field, 1, axis=0))
+        return ahead - behind
+
+    def cols(field):
+        return pltpu.roll(field, columns - 1, axis=1) - pltpu.roll(field, 1, axis=1)
+
+    def mixed(fields, m):
+        return sum(coupling[l][m] * fields[l] for l in range(3))
+
+    copies = [spill_copy, depth_copy]
+    for turn in range(STEPS):
+        step = STEPS - 1 - turn
+        state = adjoint_ref if turn == 0 else out_ref
+        height = [state[l] + forcing_ref[step * layers + l] for l in range(layers)]
+        if turn > 0:
+            for l in range(layers):
+                number = step * layers + l
+                height[l] += jnp.where(first, spill_in[number : number + 1, :], 0.0)
+        east = [state[layers + l] for l in range(layers)]
+        north = [state[2 * layers + l] for l in range(layers)]
+        east_mix = [mixed(east, m) for m in range(layers)]
+        for l in range(layers):
+            thick = depth_ref[l] * height[l]
+            edge_out[turn, 0, l : l + 1, :] = thick[0:1, :]
+            edge_out[turn, 1, l : l + 1, :] = thick[tile_rows - 1 :, :]
+            edge_out[turn, 0, layers + l : layers + l + 1, :] = east_mix[l][0:1, :]
+            edge_out[turn, 1, layers + l : layers + l + 1, :] = east_mix[l][tile_rows - 1 :, :]
+        to_before = copy(edge_out.at[turn, 0], edge_in.at[turn, 0], 2 * turn, before)
+        to_after = copy(edge_out.at[turn, 1], edge_in.at[turn, 1], 2 * turn + 1, after)
+        to_before.start()
+        to_after.start()
+        copies += [to_before, to_after]
+        if turn == 0:
+            spill_copy.wait_recv()
+            for l in range(layers):
+                number = step * layers + l
+                height[l] += jnp.where(first, spill_in[number : number + 1, :], 0.0)
+        for l in range(layers):
+            thick = depth_ref[l] * height[l]
+            north_mix = mixed(north, l)
+            out_ref[l] = height[l] + half * (rows_inside(east_mix[l]) + cols(north_mix))
+            out_ref[layers + l] = (
+                east[l]
+                + half * rows_inside(thick)
+                - time_step * (coriolis * north[l] + friction * east[l])
+            )
+            out_ref[2 * layers + l] = (
+                north[l]
+                + half * cols(thick)
+                + time_step * (coriolis * east[l] - friction * north[l])
+            )
+        to_before.wait_recv()
+        to_after.wait_recv()
+        if turn == 0:
+            depth_copy.wait_recv()
+        for l in range(layers):
+            below = edge_in[turn, 0, l : l + 1, :]
+            if turn == 0:
+                number = step * layers + l
+                below += depth_in[l : l + 1, :] * spill_ref[number : number + 1, :]
+            above = edge_in[turn, 1, l : l + 1, :]
+            below_mix = edge_in[turn, 0, layers + l : layers + l + 1, :]
+            above_mix = edge_in[turn, 1, layers + l : layers + l + 1, :]
+            out_ref[l, 0:1, :] += -half * above_mix
+            out_ref[l, tile_rows - 1 :, :] += half * below_mix
+            out_ref[layers + l, 0:1, :] += -half * above
+            out_ref[layers + l, tile_rows - 1 :, :] += half * below
+    for one in copies:
+        one.wait_send()
+
+
+def stencil(adjoint, depth, forcing, spill):
+    layers, tile_rows, columns = depth.shape
+    planes = forcing.shape[0]
+    vmem = pl.BlockSpec(memory_space=pltpu.VMEM)
+    return pl.pallas_call(
+        stencil_kernel,
+        out_shape=jax.ShapeDtypeStruct((3 * layers, tile_rows, columns), jnp.float32),
+        in_specs=[vmem] * 4,
+        out_specs=vmem,
+        scratch_shapes=[
+            pltpu.VMEM((STEPS, 2, 2 * layers, columns), jnp.float32),
+            pltpu.VMEM((STEPS, 2, 2 * layers, columns), jnp.float32),
+            pltpu.VMEM((layers, columns), jnp.float32),
+            pltpu.VMEM((layers, columns), jnp.float32),
+            pltpu.VMEM((planes, columns), jnp.float32),
+            pltpu.SemaphoreType.DMA((2 * STEPS + 2,)),
+            pltpu.SemaphoreType.DMA((2 * STEPS + 2,)),
+        ],
+        compiler_params=pltpu.CompilerParams(
+            collective_id=0, has_side_effects=True, vmem_limit_bytes=32 * 1024 * 1024
+        ),
+        name="stencil",
+    )(adjoint, depth, forcing, spill)
 
 
 def body(
@@ -324,21 +449,8 @@
     )
     arrived = lax.all_to_all(buffer, "space", split_axis=0, concat_axis=0, tiled=True)
     forcing, spill = force(arrived, planes, tile_rows, columns)
-    count = lax.axis_size("space")
-    carried = lax.ppermute(spill[:, 0], "space", [(i, (i + 1) % count) for i in range(count)])
-    forcing = forcing.at[:, 0, :].add(carried)
-    coriolis = coriolis_mid + coriolis_slope * (
-        jnp.arange(columns, dtype=jnp.float32) / columns - 0.5
-    )
     adjoint = following[0].reshape(3 * layer_count, tile_rows, columns)
-    depth_ext = padded(layer_depth, (("space", 1),), 1)
-    current = adjoint
-    for step_index in reversed(range(STEPS)):
-        current = current.at[0:layer_count].add(
-            forcing[step_index * layer_count : (step_index + 1) * layer_count]
-        )
-        extended = padded(current, (("space", 1),), 1)
-        current = advance(extended, depth_ext, coriolis, layer_count)
+    current = stencil(adjoint, layer_depth, forcing, spill)
     result = adjoint_in[0] - current.reshape(3, layer_count, tile_rows, columns)
     return result[None]
 

time: 145 us -> 92.7 us (0.64)
  the two profiles are of different devices: /device:TPU:0 before, /device:TPU:2 now
where the time goes in v2:
time: 92.7 us; the launch traced here: 92.4 us
  Pallas kernels  65.8 us (71%)
  waiting for transfers between devices  13.2 us (14%)
  starting transfers between devices  7.26 us (8%)
  local copies, waits for them, and re-layouts  4.46 us (5%)
  other arithmetic  1.02 us (1%)
    pallas_call x1, Pallas kernels, stencil(): pl.pallas_call(stencil_kernel, out_shape=jax.ShapeDtypeStruct((3 * layers...  25.3 us
    pallas_call x1, Pallas kernels, force(): pl.pallas_call(functools.partial(force_kernel, planes, tile_rows, columns...  24.3 us
    pallas_call x1, Pallas kernels, route(): pl.pallas_call(functools.partial(route_kernel, tiles, capacity, columns,...  16.2 us
    all_to_all x1, waiting for transfers between devices, body(): lax.all_to_all(buffer, 'space', split_axis=0, concat_axis=0, tiled=True)  13.2 us
    all_to_all x1, starting transfers between devices, body(): lax.all_to_all(buffer, 'space', split_axis=0, concat_axis=0, tiled=True)  5.97 us
    unnamed x14, local copies, waits for them, and re-layouts  4.31 us
  transfers between devices with their start and end apart: 2, of which 1 were waited for; matrix products, arithmetic and copies ran while one was open for 0% of the time, Pallas kernels for 26%

profile of v2, /device:TPU:2, one launch (start us, length us, event | category | flops | bytes accessed | tf_op | source)
XLA Modules:
  0.0 92.4 jit_solution(18332657795459511761)
XLA Ops:
  0.7 0.0 copy-start
  0.7 0.9 %copy-done = f32[4,1,16384]{2,1,0:T(1,128)S(1)} copy-done((f32[4,1,16384]{2,1,0:T(1,128)S(1)}, f32[4,1,16384]{2,1,0:T(1,128)}, u32[]{:S(2)}) %copy-start) | copy-done | bytes 262168
  1.6 0.0 copy-start.2
  1.6 0.8 copy-done.2
  2.4 0.0 copy-start.3
  2.4 0.8 copy-done.3
  3.3 0.0 copy-start.4
  3.3 0.8 copy-done.4
  4.1 0.0 copy-start.5
  4.1 0.8 copy-done.5
  5.0 16.2 %route.1 = f32[8,60,256]{2,1,0:T(8,128)} custom-call(s32[1,1]{1,0:T(1,128)S(6)} %copy.9.count_ref, s32[128,128]{1,0:T(8,128)S(1)} %bitcast.10, s32[128,128]{1,0:T(8,128)S(1)} %bitcast.11, s32[128,128]{1,0:T(8,128)S(1)} %bitcast.12, f32[128,128]{1,0:T(8,128)S(1)} %bitcast.13, f32[4,128,128]{2,1,0:T(8,128)S(1)} %bitcast.9), custom_call_target="tpu_custom_call" | custom-call | tf_op jit(solution)/shard_map/route/pallas_call | solution.py:156
  21.2 0.0 copy-start.6
  21.2 6.0 %all-to-all-start = ((f32[8,60,256]{2,1,0:T(8,128)}), f32[8,60,256]{2,1,0:T(8,128)S(1)}, u32[]{:S(2)}, u32[]{:S(2)}) async-start(f32[8,60,256]{2,1,0:T(8,128)} %route.1), calls=%async_computation | async-start | bytes 1048576 | tf_op jit(solution)/shard_map/all_to_all | solution.py:450
  27.1 0.0 copy-done.6
  27.1 1.3 %collective-permute-start = (f32[1,3,3,8,2048]{4,3,2,1,0:T(8,128)S(1)}, f32[1,3,3,8,2048]{4,3,2,1,0:T(8,128)S(1)}, u32[]{:S(2)}, u32[]{:S(2)}) collective-permute-start(f32[1,3,3,8,2048]{4,3,2,1,0:T(8,128)S(1)} %copy-done.6), channel_id=1, source_target_pairs={{1,0},{3,2},{5,4},{7,6},{9,8},{11,10},{13,12},{15,14},{17,16},{19,... | collective-permute-start | bytes 1769480 | tf_op jit(solution)/shard_map/ppermute | solution.py:436
  28.4 13.2 %all-to-all-done.in_ref = f32[8,60,256]{2,1,0:T(8,128)S(1)} async-done(((f32[8,60,256]{2,1,0:T(8,128)}), f32[8,60,256]{2,1,0:T(8,128)S(1)}, u32[]{:S(2)}, u32[]{:S(2)}) %all-to-all-start) | async-done | bytes 491552 | tf_op jit(solution)/shard_map/all_to_all | solution.py:450
  41.6 0.1 select_reduce_fusion
  41.8 0.1 convert_element_type.13.high_ref
  41.8 0.1 convert_element_type.11.low_ref
  41.9 0.0 copy-start.1
  41.9 24.3 %force.1 = (f32[12,8,2048]{2,1,0:T(8,128)S(1)}, f32[12,2048]{1,0:T(8,128)S(1)}) custom-call(s32[80]{0:T(128)S(1)} %convert_element_type.11.low_ref, s32[80]{0:T(128)S(1)} %convert_element_type.13.high_ref, f32[8,60,256]{2,1,0:T(8,128)S(1)} %all-to-all-done.in_ref), custom_call_target="tpu_custom_call" | custom-call | tf_op jit(solution)/shard_map/force/pallas_call | solution.py:261
  66.2 0.0 collective-permute-done
  66.2 0.0 copy-done.1
  66.3 25.3 %stencil.1 = f32[9,8,2048]{2,1,0:T(8,128)S(1)} custom-call(f32[9,8,2048]{2,1,0:T(8,128)S(1)} %bitcast.8, f32[3,8,2048]{2,1,0:T(8,128)S(1)} %copy-done.1, f32[12,8,2048]{2,1,0:T(8,128)S(1)} %get-tuple-element.7.forcing_ref, f32[12,2048]{1,0:T(8,128)S(1)} %get-tuple-element.8.spill_ref), custom_call_target="tpu_custom_call" | custom-call | tf_op jit(solution)/shard_map/stencil/pallas_call | solution.py:404
  91.5 0.9 sub.4
  (1 shorter events, 0.0 us)
Async XLA Ops:
  0.7 1.0 %copy-start = (f32[4,1,16384]{2,1,0:T(1,128)S(1)}, f32[4,1,16384]{2,1,0:T(1,128)}, u32[]{:S(2)}) copy-start(f32[4,1,16384]{2,1,0:T(1,128)} %param.14) | copy-start | bytes 786436
  1.6 0.8 copy-start.2
  2.4 0.8 copy-start.3
  3.3 0.8 copy-start.4
  4.1 0.8 copy-start.5
  21.2 6.0 %copy-start.6 = (f32[1,3,3,8,2048]{4,3,2,1,0:T(8,128)S(1)}, f32[1,3,3,8,2048]{4,3,2,1,0:T(8,128)}, u32[]{:S(2)}) copy-start(f32[1,3,3,8,2048]{4,3,2,1,0:T(8,128)} %param.8) | copy-start | bytes 1769476
  21.2 20.5 %all-to-all-start = ((f32[8,60,256]{2,1,0:T(8,128)}), f32[8,60,256]{2,1,0:T(8,128)S(1)}, u32[]{:S(2)}, u32[]{:S(2)}) async-start(f32[8,60,256]{2,1,0:T(8,128)} %route.1), calls=%async_computation | async-start | bytes 1048576 | tf_op jit(solution)/shard_map/all_to_all | solution.py:450
  27.1 39.1 %collective-permute-start = (f32[1,3,3,8,2048]{4,3,2,1,0:T(8,128)S(1)}, f32[1,3,3,8,2048]{4,3,2,1,0:T(8,128)S(1)}, u32[]{:S(2)}, u32[]{:S(2)}) collective-permute-start(f32[1,3,3,8,2048]{4,3,2,1,0:T(8,128)S(1)} %copy-done.6), channel_id=1, source_target_pairs={{1,0},{3,2},{5,4},{7,6},{9,8},{11,10},{13,12},{15,14},{17,16},{19,... | collective-permute-start | bytes 1769480 | tf_op jit(solution)/shard_map/ppermute | solution.py:436
  41.9 24.3 %copy-start.1 = (f32[3,8,2048]{2,1,0:T(8,128)S(1)}, f32[3,8,2048]{2,1,0:T(8,128)}, u32[]{:S(2)}) copy-start(f32[3,8,2048]{2,1,0:T(8,128)} %depth_ref.1) | copy-start | bytes 589828

commit v3 on v2

--- a/solution.py
+++ b/solution.py
@@ -39,17 +39,78 @@
     tile_rows,
     width,
     count_ref,
+    cell_hbm,
+    plane_hbm,
+    owner_hbm,
+    innov_hbm,
+    weight_hbm,
+    adjoint_hbm,
+    out_ref,
+    following_hbm,
     cell_ref,
     plane_ref,
     owner_ref,
     innov_ref,
     weight_ref,
-    out_ref,
     key_ref,
     pos_ref,
     piece_ref,
+    hit_ref,
     acc_ref,
+    slab_ref,
+    load_sem,
+    send_sem,
+    recv_sem,
 ):
+    loads = [
+        pltpu.make_async_copy(source, target, load_sem.at[number])
+        for number, (source, target) in enumerate(
+            [
+                (cell_hbm, cell_ref),
+                (owner_hbm, owner_ref),
+                (plane_hbm, plane_ref),
+                (innov_hbm, innov_ref),
+                (weight_hbm, weight_ref),
+            ]
+        )
+    ]
+    for load in loads:
+        load.start()
+    me = lax.axis_index("space")
+    window = lax.axis_index("tm")
+    windows = lax.axis_size("tm")
+    half = tiles // 2
+    local = lax.rem(me, half)
+    my_base = me - local
+    other_base = half - my_base
+    barrier = pltpu.get_barrier_semaphore()
+    for distance in range(1, tiles):
+        pl.semaphore_signal(
+            barrier,
+            inc=1,
+            device_id={"space": lax.rem(me + distance, tiles)},
+            device_id_type=pl.DeviceIdType.MESH,
+        )
+    earlier_window = lax.rem(window + windows - 1, windows)
+    for distance in range(1, windows):
+        pl.semaphore_signal(
+            barrier,
+            inc=1,
+            device_id={"tm": lax.rem(window + distance, windows)},
+            device_id_type=pl.DeviceIdType.MESH,
+        )
+    pl.semaphore_wait(barrier, tiles - 1 + windows - 1)
+    follow = pltpu.make_async_remote_copy(
+        src_ref=adjoint_hbm,
+        dst_ref=following_hbm,
+        send_sem=send_sem.at[tiles],
+        recv_sem=recv_sem.at[tiles],
+        device_id={"tm": earlier_window},
+        device_id_type=pl.DeviceIdType.MESH,
+    )
+    follow.start()
+    for load in loads:
+        load.wait()
     lines = cell_ref.shape[0]
     buckets = columns // WINDOW
     keys = tiles * buckets
@@ -112,61 +173,128 @@
         return base
 
     lax.fori_loop(0, lines // 8, rank_step, base)
-    acc_ref[...] = jnp.zeros_like(acc_ref)
     log_width = width.bit_length() - 1
-
-    def move_step(step, carry):
-        span = range(8)
-        slots, lefts = [], []
-        for extra in span:
-            position = pos_ref[pl.ds(step * 8 + extra, 1), :]
-            slots.append(one_hot(jnp.right_shift(position, log_width), slot_rows).astype(jnp.bfloat16))
-            lefts.append(one_hot(jnp.bitwise_and(position, width - 1), width).astype(jnp.bfloat16))
-        lane_hits = jnp.concatenate(lefts, axis=1)
-        parts = []
-        for extra in span:
-            pieces = [
-                slots[extra] * spread(piece_ref[piece, pl.ds(step * 8 + extra, 1), :], slot_rows)
-                for piece in range(11)
-            ]
-            parts.append(jnp.concatenate(pieces, axis=0))
-        acc_ref[...] += lax.dot_general(
-            jnp.concatenate(parts, axis=1), lane_hits, NT, preferred_element_type=jnp.float32
-        )
-        return carry
-
-    lax.fori_loop(0, lines // 8, move_step, 0)
+    half_rows = slot_rows // 2
+    part_rows = (half_rows + 15) // 16 * 16
     per_owner = capacity // width
-    for owner in range(tiles):
-        for field in range(FIELDS):
-
-            def piece_rows(piece):
-                first = piece * slot_rows + owner * per_owner
-                return acc_ref[first : first + per_owner, :]
-
-            value = piece_rows(0) if field == 0 else piece_rows(2 * field - 1) + piece_rows(2 * field)
-            out_ref[owner, field * per_owner : (field + 1) * per_owner, :] = value
-
-
-def route(cell, plane, owner, innovation, weights, count, tiles, capacity, columns, tile_rows):
+    per_half = tiles // 2
+    span = range(8)
+
+    def move_half(first_row, fresh):
+        acc_ref[...] = jnp.zeros_like(acc_ref)
+
+        def move_step(step, carry):
+            parts, lefts = [], []
+            for extra in span:
+                position = pos_ref[pl.ds(step * 8 + extra, 1), :]
+                slot = jnp.right_shift(position, log_width) - first_row
+                slots = one_hot(slot, part_rows).astype(jnp.bfloat16)
+                pieces = [
+                    slots * spread(piece_ref[piece, pl.ds(step * 8 + extra, 1), :], part_rows)
+                    for piece in range(11)
+                ]
+                parts.append(jnp.concatenate(pieces, axis=0))
+                if fresh:
+                    lane = jnp.bitwise_and(position, width - 1)
+                    lefts.append(one_hot(lane, width).astype(jnp.bfloat16))
+            if fresh:
+                lane_hits = jnp.concatenate(lefts, axis=1)
+                hit_ref[step] = lane_hits
+            else:
+                lane_hits = hit_ref[step]
+            acc_ref[...] += lax.dot_general(
+                jnp.concatenate(parts, axis=1), lane_hits, NT, preferred_element_type=jnp.float32
+            )
+            return carry
+
+        lax.fori_loop(0, lines // 8, move_step, 0)
+        for owner in range(per_half):
+            for field in range(FIELDS):
+
+                def piece_rows(piece):
+                    first = piece * part_rows + owner * per_owner
+                    return acc_ref[first : first + per_owner, :]
+
+                value = piece_rows(0)
+                if field > 0:
+                    value = piece_rows(2 * field - 1) + piece_rows(2 * field)
+                target = slice(field * per_owner, (field + 1) * per_owner)
+                slab_ref[0 if fresh else 1, owner, target, :] = value
+
+    def exchange(base, group, number):
+        to_local = lax.rem(local + number, half)
+        from_tile = base + lax.rem(local + half - number, half)
+
+        def copy(slot):
+            return pltpu.make_async_remote_copy(
+                src_ref=slab_ref.at[group, to_local],
+                dst_ref=out_ref.at[slot],
+                send_sem=send_sem.at[group * half + number],
+                recv_sem=recv_sem.at[group * half + number],
+                device_id={"space": base + to_local},
+                device_id_type=pl.DeviceIdType.MESH,
+            )
+
+        return copy(me), copy(from_tile)
+
+    pairs = []
+    move_half(other_base * per_owner, True)
+    for number in range(half):
+        pairs.append(exchange(other_base, 0, number))
+        pairs[-1][0].start()
+    move_half(my_base * per_owner, False)
+    for number in range(1, half):
+        pairs.append(exchange(my_base, 1, number))
+        pairs[-1][0].start()
+    out_ref[me] = slab_ref[1, local]
+    for sent, got in pairs:
+        got.wait_recv()
+    follow.wait_recv()
+    for sent, got in pairs:
+        sent.wait_send()
+    follow.wait_send()
+
+
+def route(
+    cell, plane, owner, innov, weights, count, adjoint, tiles, capacity, columns, tile_rows
+):
     lines = cell.shape[0]
     width = 256 if capacity % 256 == 0 else LANES
-    slot_rows = tiles * capacity // width
+    half_rows = tiles * capacity // width // 2
+    part_rows = (half_rows + 15) // 16 * 16
+    depth = FIELDS * (capacity // width)
     vmem = pl.BlockSpec(memory_space=pltpu.VMEM)
+    anywhere = pl.BlockSpec(memory_space=pl.ANY)
+    whole = pltpu.VMEM((lines, LANES), jnp.int32)
     return pl.pallas_call(
         functools.partial(route_kernel, tiles, capacity, columns, tile_rows, width),
-        out_shape=jax.ShapeDtypeStruct((tiles, FIELDS * (capacity // width), width), jnp.float32),
-        in_specs=[pl.BlockSpec(memory_space=pltpu.SMEM)] + [vmem] * 5,
-        out_specs=vmem,
+        out_shape=(
+            jax.ShapeDtypeStruct((tiles, depth, width), jnp.float32),
+            jax.ShapeDtypeStruct(adjoint.shape, adjoint.dtype),
+        ),
+        in_specs=[pl.BlockSpec(memory_space=pltpu.SMEM)] + [anywhere] * 6,
+        out_specs=(vmem, anywhere),
         scratch_shapes=[
-            pltpu.VMEM((lines, LANES), jnp.int32),
-            pltpu.VMEM((lines, LANES), jnp.int32),
+            whole,
+            whole,
+            whole,
+            pltpu.VMEM((lines, LANES), jnp.float32),
+            pltpu.VMEM((4, lines, LANES), jnp.float32),
+            whole,
+            whole,
             pltpu.VMEM((11, lines, LANES), jnp.float32),
-            pltpu.VMEM((11 * slot_rows, width), jnp.float32),
+            pltpu.VMEM((lines // 8, width, 8 * LANES), jnp.bfloat16),
+            pltpu.VMEM((11 * part_rows, width), jnp.float32),
+            pltpu.VMEM((2, tiles // 2, depth, width), jnp.float32),
+            pltpu.SemaphoreType.DMA((5,)),
+            pltpu.SemaphoreType.DMA((tiles + 1,)),
+            pltpu.SemaphoreType.DMA((tiles + 1,)),
         ],
-        compiler_params=pltpu.CompilerParams(vmem_limit_bytes=48 * 1024 * 1024),
+        compiler_params=pltpu.CompilerParams(
+            collective_id=1, has_side_effects=True, vmem_limit_bytes=48 * 1024 * 1024
+        ),
         name="route",
-    )(count, cell, plane, owner, innovation, weights)
+    )(count, cell, plane, owner, innov, weights, adjoint)
 
 
 def force_kernel(
@@ -335,17 +463,22 @@
     def mixed(fields, m):
         return sum(coupling[l][m] * fields[l] for l in range(3))
 
+    goes_on = jnp.where(lax.axis_index("tm") == lax.axis_size("tm") - 1, 0, 1)
+
+    def started(number):
+        return jnp.where(goes_on > 0, adjoint_ref[number], 0.0)
+
     copies = [spill_copy, depth_copy]
     for turn in range(STEPS):
         step = STEPS - 1 - turn
-        state = adjoint_ref if turn == 0 else out_ref
-        height = [state[l] + forcing_ref[step * layers + l] for l in range(layers)]
+        state = started if turn == 0 else out_ref.__getitem__
+        height = [state(l) + forcing_ref[step * layers + l] for l in range(layers)]
         if turn > 0:
             for l in range(layers):
                 number = step * layers + l
                 height[l] += jnp.where(first, spill_in[number : number + 1, :], 0.0)
-        east = [state[layers + l] for l in range(layers)]
-        north = [state[2 * layers + l] for l in range(layers)]
+        east = [state(layers + l) for l in range(layers)]
+        north = [state(2 * layers + l) for l in range(layers)]
         east_mix = [mixed(east, m) for m in range(layers)]
         for l in range(layers):
             thick = depth_ref[l] * height[l]
@@ -432,25 +565,23 @@
     obs_rows = obs_cell.shape[1]
     capacity = 5 * obs_rows // (4 * tiles)
     planes = STEPS * layer_count
-    windows = lax.axis_size("tm")
-    following = lax.ppermute(adjoint_in, "tm", [(i + 1, i) for i in range(windows - 1)])
     lines = obs_rows // LANES
-    buffer = route(
+    adjoint = adjoint_in[0].reshape(3 * layer_count, tile_rows, columns)
+    arrived, following = route(
         obs_cell.reshape(lines, LANES),
         obs_plane.reshape(lines, LANES),
         obs_owner.reshape(lines, LANES),
         innovation.reshape(lines, LANES),
         obs_weight.reshape(4, lines, LANES),
         obs_count,
+        adjoint,
         tiles,
         capacity,
         columns,
         tile_rows,
     )
-    arrived = lax.all_to_all(buffer, "space", split_axis=0, concat_axis=0, tiled=True)
     forcing, spill = force(arrived, planes, tile_rows, columns)
-    adjoint = following[0].reshape(3 * layer_count, tile_rows, columns)
-    current = stencil(adjoint, layer_depth, forcing, spill)
+    current = stencil(following, layer_depth, forcing, spill)
     result = adjoint_in[0] - current.reshape(3, layer_count, tile_rows, columns)
     return result[None]
 

time: 92.7 us -> 87.9 us (0.948)
  the two profiles are of different devices: /device:TPU:2 before, /device:TPU:0 now
where the time goes in v3:
time: 87.9 us; the launch traced here: 86.6 us
  Pallas kernels  79.4 us (90%)
  local copies, waits for them, and re-layouts  5.53 us (6%)
  other arithmetic  1 us (1%)
    pallas_call x1, Pallas kernels, route(): pl.pallas_call(functools.partial(route_kernel, tiles, capacity, columns,...  33.2 us
    pallas_call x1, Pallas kernels, force(): pl.pallas_call(functools.partial(force_kernel, planes, tile_rows, columns...  23.6 us
    pallas_call x1, Pallas kernels, stencil(): pl.pallas_call(stencil_kernel, out_shape=jax.ShapeDtypeStruct((3 * layers...  22.6 us
    unnamed x16, local copies, waits for them, and re-layouts  5.37 us

profile of v3, /device:TPU:0, one launch (start us, length us, event | category | flops | bytes accessed | tf_op | source)
XLA Modules:
  0.0 86.6 jit_solution(14408326611293486401)
XLA Ops:
  0.7 0.0 copy-start
  0.7 1.1 %copy-done = f32[1,3,3,8,2048]{4,3,2,1,0:T(8,128)S(1)} copy-done((f32[1,3,3,8,2048]{4,3,2,1,0:T(8,128)S(1)}, f32[1,3,3,8,2048]{4,3,2,1,0:T(8,128)}, u32[]{:S(2)}) %copy-start) | copy-done | bytes 589848
  1.7 0.0 copy-start.2
  1.7 0.9 %copy-done.2 = f32[4,1,16384]{2,1,0:T(1,128)S(1)} copy-done((f32[4,1,16384]{2,1,0:T(1,128)S(1)}, f32[4,1,16384]{2,1,0:T(1,128)}, u32[]{:S(2)}) %copy-start.2) | copy-done | bytes 262168
  2.7 0.0 copy-start.4
  2.7 0.8 copy-done.4
  3.5 0.0 copy-start.5
  3.5 0.8 copy-done.5
  4.3 0.0 copy-start.6
  4.4 0.8 copy-done.6
  5.2 0.0 copy-start.7
  5.2 0.8 copy-done.7
  6.0 33.2 %route.1 = (f32[8,60,256]{2,1,0:T(8,128)S(1)}, f32[9,8,2048]{2,1,0:T(8,128)S(1)}) custom-call(s32[1,1]{1,0:T(1,128)S(6)} %copy.9.count_ref, s32[128,128]{1,0:T(8,128)S(1)} %bitcast.10, s32[128,128]{1,0:T(8,128)S(1)} %bitcast.11, s32[128,128]{1,0:T(8,128)S(1)} %bitcast.12, f32[128,128]{1,0:T(8,128)S(1)} %bitcast.13, f32[4,128,128]{2,1,0:T(8,128)S(1)} %bitcast.9, ...), custom_call_target="tpu_custom_call" | custom-call | tf_op jit(solution)/shard_map/route/pallas_call | solution.py:269
  39.2 0.1 select_reduce_fusion
  39.4 0.1 convert_element_type.13.high_ref
  39.4 0.1 convert_element_type.11.low_ref
  39.5 0.0 copy-start.3
  39.5 23.6 %force.1 = (f32[12,8,2048]{2,1,0:T(8,128)S(1)}, f32[12,2048]{1,0:T(8,128)S(1)}) custom-call(s32[80]{0:T(128)S(1)} %convert_element_type.11.low_ref, s32[80]{0:T(128)S(1)} %convert_element_type.13.high_ref, f32[8,60,256]{2,1,0:T(8,128)S(1)} %get-tuple-element.10.in_ref), custom_call_target="tpu_custom_call" | custom-call | tf_op jit(solution)/shard_map/force/pallas_call | solution.py:389
  63.1 0.0 copy-done.3
  63.1 0.0 copy-start.1
  63.1 22.6 %stencil.1 = f32[9,8,2048]{2,1,0:T(8,128)S(1)} custom-call(f32[9,8,2048]{2,1,0:T(8,128)S(1)} %get-tuple-element.9.adjoint_ref, f32[3,8,2048]{2,1,0:T(8,128)S(1)} %copy-done.3, f32[12,8,2048]{2,1,0:T(8,128)S(1)} %get-tuple-element.11.forcing_ref, f32[12,2048]{1,0:T(8,128)S(1)} %get-tuple-element.12.spill_ref), custom_call_target="tpu_custom_call" | custom-call | tf_op jit(solution)/shard_map/stencil/pallas_call | solution.py:537
  85.7 0.0 copy-done.1
  85.7 0.9 %sub.4 = f32[1,3,3,8,2048]{4,3,2,1,0:T(8,128)} subtract(f32[1,3,3,8,2048]{4,3,2,1,0:T(8,128)S(1)} %copy-done.1, f32[1,3,3,8,2048]{4,3,2,1,0:T(8,128)S(1)} %bitcast.7) | non-fusion elementwise | flops 147456 | bytes 1769472 | tf_op jit(solution)/shard_map/sub | solution.py:585
  (1 shorter events, 0.0 us)
Async XLA Ops:
  0.7 1.1 %copy-start = (f32[1,3,3,8,2048]{4,3,2,1,0:T(8,128)S(1)}, f32[1,3,3,8,2048]{4,3,2,1,0:T(8,128)}, u32[]{:S(2)}) copy-start(f32[1,3,3,8,2048]{4,3,2,1,0:T(8,128)} %param.8) | copy-start | bytes 1769476
  1.7 0.9 %copy-start.2 = (f32[4,1,16384]{2,1,0:T(1,128)S(1)}, f32[4,1,16384]{2,1,0:T(1,128)}, u32[]{:S(2)}) copy-start(f32[4,1,16384]{2,1,0:T(1,128)} %param.14) | copy-start | bytes 786436
  2.7 0.8 copy-start.4
  3.5 0.8 copy-start.5
  4.3 0.8 copy-start.6
  5.2 0.8 copy-start.7
  39.5 23.6 %copy-start.3 = (f32[3,8,2048]{2,1,0:T(8,128)S(1)}, f32[3,8,2048]{2,1,0:T(8,128)}, u32[]{:S(2)}) copy-start(f32[3,8,2048]{2,1,0:T(8,128)} %depth_ref.1) | copy-start | bytes 589828
  63.1 22.6 %copy-start.1 = (f32[1,3,3,8,2048]{4,3,2,1,0:T(8,128)S(1)}, f32[1,3,3,8,2048]{4,3,2,1,0:T(8,128)}, u32[]{:S(2)}) copy-start(f32[1,3,3,8,2048]{4,3,2,1,0:T(8,128)} %param.8) | copy-start | bytes 1769476

commit v4 on v3

--- a/solution.py
+++ b/solution.py
@@ -11,7 +11,7 @@
 LANES = 128
 WINDOW = 256
 FIELDS = 6
-GROUP = 4
+GROUP = 8
 
 time_step = 0.4
 friction = 0.05
@@ -30,6 +30,13 @@
 def one_hot(index_row, rows):
     places = lax.broadcasted_iota(jnp.int32, (rows, index_row.shape[1]), 0)
     return jnp.where(places == index_row, 1.0, 0.0)
+
+
+def one_hot_16(index_row, rows):
+    places = lax.broadcasted_iota(jnp.int32, (rows, index_row.shape[1]), 0)
+    places = places.astype(jnp.float32).astype(jnp.bfloat16)
+    same = places == spread(index_row.astype(jnp.float32), rows)
+    return jnp.where(same, jnp.bfloat16(1), jnp.bfloat16(0))
 
 
 def route_kernel(
@@ -188,7 +195,7 @@
             for extra in span:
                 position = pos_ref[pl.ds(step * 8 + extra, 1), :]
                 slot = jnp.right_shift(position, log_width) - first_row
-                slots = one_hot(slot, part_rows).astype(jnp.bfloat16)
+                slots = one_hot_16(slot, part_rows)
                 pieces = [
                     slots * spread(piece_ref[piece, pl.ds(step * 8 + extra, 1), :], part_rows)
                     for piece in range(11)
@@ -196,7 +203,7 @@
                 parts.append(jnp.concatenate(pieces, axis=0))
                 if fresh:
                     lane = jnp.bitwise_and(position, width - 1)
-                    lefts.append(one_hot(lane, width).astype(jnp.bfloat16))
+                    lefts.append(one_hot_16(lane, width))
             if fresh:
                 lane_hits = jnp.concatenate(lefts, axis=1)
                 hit_ref[step] = lane_hits
@@ -264,7 +271,7 @@
     part_rows = (half_rows + 15) // 16 * 16
     depth = FIELDS * (capacity // width)
     vmem = pl.BlockSpec(memory_space=pltpu.VMEM)
-    anywhere = pl.BlockSpec(memory_space=pl.ANY)
+    anywhere = pl.BlockSpec(memory_space=pltpu.HBM)
     whole = pltpu.VMEM((lines, LANES), jnp.int32)
     return pl.pallas_call(
         functools.partial(route_kernel, tiles, capacity, columns, tile_rows, width),
@@ -336,7 +343,7 @@
 
         line = field(0).astype(jnp.int32) - 1
         column = field(1).astype(jnp.int32)
-        line_hits = one_hot(line, cells).astype(jnp.bfloat16)
+        line_hits = one_hot_16(line, cells)
         highs, lows = [], []
         for corner in range(4):
             value = field(2 + corner)
@@ -346,7 +353,7 @@
         left = jnp.concatenate(
             [jnp.concatenate(highs, axis=0), jnp.concatenate(lows, axis=0)], axis=1
         )
-        hits = one_hot(column - item_ref[2, item] * WINDOW, WINDOW).astype(jnp.bfloat16)
+        hits = one_hot_16(column - item_ref[2, item] * WINDOW, WINDOW)
         right = jnp.concatenate([hits, hits], axis=1)
         return lax.dot_general(left, right, NT, preferred_element_type=jnp.float32)
 

time: 87.9 us -> 85.4 us (0.972); the launches traced: 86.6 us -> 85.7 us
  Pallas kernels: 79.4 us -> 78.5 us
    pallas_call x1, Pallas kernels: 22.6 us -> 30.2 us  [stencil(): pl.pallas_call(stencil_kernel, out_shape=jax.ShapeDtypeStruct((3 * layers...]
    pallas_call x1, Pallas kernels: 23.6 us -> 16 us  [force(): pl.pallas_call(functools.partial(force_kernel, planes, tile_rows, columns...]
    pallas_call x1, Pallas kernels: 33.2 us -> 32.2 us  [route(): pl.pallas_call(functools.partial(route_kernel, tiles, capacity, columns,...]
where the time goes in v4:
time: 85.4 us; the launch traced here: 85.7 us
  Pallas kernels  78.5 us (92%)
  local copies, waits for them, and re-layouts  5.53 us (6%)
  other arithmetic  1 us (1%)
    pallas_call x1, Pallas kernels, route(): pl.pallas_call(functools.partial(route_kernel, tiles, capacity, columns,...  32.2 us
    pallas_call x1, Pallas kernels, stencil(): pl.pallas_call(stencil_kernel, out_shape=jax.ShapeDtypeStruct((3 * layers...  30.2 us
    pallas_call x1, Pallas kernels, force(): pl.pallas_call(functools.partial(force_kernel, planes, tile_rows, columns...  16 us
    unnamed x16, local copies, waits for them, and re-layouts  5.37 us

profile of v4, /device:TPU:0, one launch (start us, length us, event | category | flops | bytes accessed | tf_op | source)
XLA Modules:
  0.0 85.7 jit_solution(16354020209160276056)
XLA Ops:
  0.7 0.0 copy-start
  0.7 1.1 %copy-done = f32[1,3,3,8,2048]{4,3,2,1,0:T(8,128)S(1)} copy-done((f32[1,3,3,8,2048]{4,3,2,1,0:T(8,128)S(1)}, f32[1,3,3,8,2048]{4,3,2,1,0:T(8,128)}, u32[]{:S(2)}) %copy-start) | copy-done | bytes 589848
  1.7 0.0 copy-start.2
  1.7 0.9 %copy-done.2 = f32[4,1,16384]{2,1,0:T(1,128)S(1)} copy-done((f32[4,1,16384]{2,1,0:T(1,128)S(1)}, f32[4,1,16384]{2,1,0:T(1,128)}, u32[]{:S(2)}) %copy-start.2) | copy-done | bytes 262168
  2.7 0.0 copy-start.4
  2.7 0.8 copy-done.4
  3.5 0.0 copy-start.5
  3.5 0.8 copy-done.5
  4.3 0.0 copy-start.6
  4.4 0.8 copy-done.6
  5.2 0.0 copy-start.7
  5.2 0.8 copy-done.7
  6.0 32.2 %route.1 = (f32[8,60,256]{2,1,0:T(8,128)S(1)}, f32[9,8,2048]{2,1,0:T(8,128)S(1)}) custom-call(s32[1,1]{1,0:T(1,128)S(6)} %copy.9.count_ref, s32[128,128]{1,0:T(8,128)S(1)} %bitcast.10, s32[128,128]{1,0:T(8,128)S(1)} %bitcast.11, s32[128,128]{1,0:T(8,128)S(1)} %bitcast.12, f32[128,128]{1,0:T(8,128)S(1)} %bitcast.13, f32[4,128,128]{2,1,0:T(8,128)S(1)} %bitcast.9, ...), custom_call_target="tpu_custom_call" | custom-call | tf_op jit(solution)/shard_map/route/pallas_call | solution.py:276
  38.2 0.1 select_reduce_fusion
  38.4 0.1 convert_element_type.13.high_ref
  38.5 0.1 convert_element_type.11.low_ref
  38.5 0.0 copy-start.3
  38.5 16.0 %force.1 = (f32[12,8,2048]{2,1,0:T(8,128)S(1)}, f32[12,2048]{1,0:T(8,128)S(1)}) custom-call(s32[80]{0:T(128)S(1)} %convert_element_type.11.low_ref, s32[80]{0:T(128)S(1)} %convert_element_type.13.high_ref, f32[8,60,256]{2,1,0:T(8,128)S(1)} %get-tuple-element.10.in_ref), custom_call_target="tpu_custom_call" | custom-call | tf_op jit(solution)/shard_map/force/pallas_call | solution.py:396
  54.6 0.0 copy-done.3
  54.6 0.0 copy-start.1
  54.6 30.2 %stencil.1 = f32[9,8,2048]{2,1,0:T(8,128)S(1)} custom-call(f32[9,8,2048]{2,1,0:T(8,128)S(1)} %get-tuple-element.9.adjoint_ref, f32[3,8,2048]{2,1,0:T(8,128)S(1)} %copy-done.3, f32[12,8,2048]{2,1,0:T(8,128)S(1)} %get-tuple-element.11.forcing_ref, f32[12,2048]{1,0:T(8,128)S(1)} %get-tuple-element.12.spill_ref), custom_call_target="tpu_custom_call" | custom-call | tf_op jit(solution)/shard_map/stencil/pallas_call | solution.py:544
  84.9 0.0 copy-done.1
  84.9 0.9 %sub.4 = f32[1,3,3,8,2048]{4,3,2,1,0:T(8,128)} subtract(f32[1,3,3,8,2048]{4,3,2,1,0:T(8,128)S(1)} %copy-done.1, f32[1,3,3,8,2048]{4,3,2,1,0:T(8,128)S(1)} %bitcast.7) | non-fusion elementwise | flops 147456 | bytes 1769472 | tf_op jit(solution)/shard_map/sub | solution.py:592
  (1 shorter events, 0.0 us)
Async XLA Ops:
  0.7 1.1 %copy-start = (f32[1,3,3,8,2048]{4,3,2,1,0:T(8,128)S(1)}, f32[1,3,3,8,2048]{4,3,2,1,0:T(8,128)}, u32[]{:S(2)}) copy-start(f32[1,3,3,8,2048]{4,3,2,1,0:T(8,128)} %param.8) | copy-start | bytes 1769476
  1.7 0.9 %copy-start.2 = (f32[4,1,16384]{2,1,0:T(1,128)S(1)}, f32[4,1,16384]{2,1,0:T(1,128)}, u32[]{:S(2)}) copy-start(f32[4,1,16384]{2,1,0:T(1,128)} %param.14) | copy-start | bytes 786436
  2.7 0.8 copy-start.4
  3.5 0.8 copy-start.5
  4.3 0.8 copy-start.6
  5.2 0.8 copy-start.7
  38.5 16.0 %copy-start.3 = (f32[3,8,2048]{2,1,0:T(8,128)S(1)}, f32[3,8,2048]{2,1,0:T(8,128)}, u32[]{:S(2)}) copy-start(f32[3,8,2048]{2,1,0:T(8,128)} %depth_ref.1) | copy-start | bytes 589828
  54.6 30.3 %copy-start.1 = (f32[1,3,3,8,2048]{4,3,2,1,0:T(8,128)S(1)}, f32[1,3,3,8,2048]{4,3,2,1,0:T(8,128)}, u32[]{:S(2)}) copy-start(f32[1,3,3,8,2048]{4,3,2,1,0:T(8,128)} %param.8) | copy-start | bytes 1769476

commit v5 on v4

--- a/solution.py
+++ b/solution.py
@@ -298,7 +298,7 @@
             pltpu.SemaphoreType.DMA((tiles + 1,)),
         ],
         compiler_params=pltpu.CompilerParams(
-            collective_id=1, has_side_effects=True, vmem_limit_bytes=48 * 1024 * 1024
+            collective_id=1, has_side_effects=True, vmem_limit_bytes=62 * 1024 * 1024
         ),
         name="route",
     )(count, cell, plane, owner, innov, weights, adjoint)

time: 85.4 us -> 82.5 us (0.966); the launches traced: 85.7 us -> 81.9 us
  local copies, waits for them, and re-layouts: 5.53 us -> 2.27 us
  Pallas kernels: 78.5 us -> 76.9 us
  other arithmetic: 1 us -> 2.01 us
    pallas_call x1, Pallas kernels: 30.2 us -> 23.4 us  [stencil(): pl.pallas_call(stencil_kernel, out_shape=jax.ShapeDtypeStruct((3 * layers...]
    pallas_call x1, Pallas kernels: 16 us -> 20.8 us  [force(): pl.pallas_call(functools.partial(force_kernel, planes, tile_rows, columns...]
    unnamed x16 -> x8, local copies, waits for them, and re-layouts: 5.37 us -> 2.11 us
    reduce_max x1, other arithmetic: 0.12 us -> 1.12 us  [force(): jnp.max(jnp.where(line > 0, column, -1.0), axis=2).reshape(tiles * per_tile)]
where the time goes in v5:
time: 82.5 us; the launch traced here: 81.9 us
  Pallas kernels  76.9 us (93%)
  local copies, waits for them, and re-layouts  2.27 us (3%)
  other arithmetic  2.01 us (2%)
    pallas_call x1, Pallas kernels, route(): pl.pallas_call(functools.partial(route_kernel, tiles, capacity, columns,...  32.7 us
    pallas_call x1, Pallas kernels, stencil(): pl.pallas_call(stencil_kernel, out_shape=jax.ShapeDtypeStruct((3 * layers...  23.4 us
    pallas_call x1, Pallas kernels, force(): pl.pallas_call(functools.partial(force_kernel, planes, tile_rows, columns...  20.8 us
    unnamed x8, local copies, waits for them, and re-layouts  2.11 us

profile of v5, /device:TPU:0, one launch (start us, length us, event | category | flops | bytes accessed | tf_op | source)
XLA Modules:
  0.0 81.9 jit_solution(9084609002824415389)
XLA Ops:
  0.7 32.7 %route.1 = (f32[8,60,256]{2,1,0:T(8,128)}, f32[9,8,2048]{2,1,0:T(8,128)}) custom-call(s32[1,1]{1,0:T(1,128)S(6)} %copy.9.count_ref, s32[128,128]{1,0:T(8,128)} %bitcast.10, s32[128,128]{1,0:T(8,128)} %bitcast.11, s32[128,128]{1,0:T(8,128)} %bitcast.12, f32[128,128]{1,0:T(8,128)} %bitcast.13, f32[4,128,128]{2,1,0:T(8,128)} %bitcast.9, f32[9,8,2048]{2,1,0:T(8,128)} %bitcast.8), custom_call_target="tpu_custom_call" | custom-call | tf_op jit(solution)/shard_map/route/pallas_call | solution.py:276
  33.4 1.1 %select_reduce_fusion = (f32[8,10]{1,0:T(8,128)S(1)}, f32[8,10]{1,0:T(8,128)S(1)}) fusion(f32[8,60,256]{2,1,0:T(8,128)} %get-tuple-element.10.in_ref), kind=kLoop, calls=%fused_computation | loop fusion | flops 102240 | bytes 164480 | tf_op jit(solution)/shard_map/reduce_max | solution.py:390
  34.5 0.1 convert_element_type.13.high_ref
  34.6 0.1 convert_element_type.11.low_ref
  34.7 0.0 copy-start
  34.7 1.0 %copy-done = f32[8,60,256]{2,1,0:T(8,128)S(1)} copy-done((f32[8,60,256]{2,1,0:T(8,128)S(1)}, f32[8,60,256]{2,1,0:T(8,128)}, u32[]{:S(2)}) %copy-start) | copy-done | bytes 491544
  35.7 0.0 copy-start.2
  35.7 20.8 %force.1 = (f32[12,8,2048]{2,1,0:T(8,128)S(1)}, f32[12,2048]{1,0:T(8,128)S(1)}) custom-call(s32[80]{0:T(128)S(1)} %convert_element_type.11.low_ref, s32[80]{0:T(128)S(1)} %convert_element_type.13.high_ref, f32[8,60,256]{2,1,0:T(8,128)S(1)} %copy-done), custom_call_target="tpu_custom_call" | custom-call | tf_op jit(solution)/shard_map/force/pallas_call | solution.py:396
  56.5 0.0 copy-done.2
  56.5 0.0 copy-start.1
  56.6 1.1 %copy-done.1 = f32[9,8,2048]{2,1,0:T(8,128)S(1)} copy-done((f32[9,8,2048]{2,1,0:T(8,128)S(1)}, f32[9,8,2048]{2,1,0:T(8,128)}, u32[]{:S(2)}) %copy-start.1) | copy-done | bytes 589848
  57.6 0.0 copy-start.3
  57.6 23.4 %stencil.1 = f32[9,8,2048]{2,1,0:T(8,128)S(1)} custom-call(f32[9,8,2048]{2,1,0:T(8,128)S(1)} %copy-done.1, f32[3,8,2048]{2,1,0:T(8,128)S(1)} %copy-done.2, f32[12,8,2048]{2,1,0:T(8,128)S(1)} %get-tuple-element.11.forcing_ref, f32[12,2048]{1,0:T(8,128)S(1)} %get-tuple-element.12.spill_ref), custom_call_target="tpu_custom_call" | custom-call | tf_op jit(solution)/shard_map/stencil/pallas_call | solution.py:544
  81.0 0.0 copy-done.3
  81.0 0.9 %sub.4 = f32[1,3,3,8,2048]{4,3,2,1,0:T(8,128)} subtract(f32[1,3,3,8,2048]{4,3,2,1,0:T(8,128)S(1)} %copy-done.3, f32[1,3,3,8,2048]{4,3,2,1,0:T(8,128)S(1)} %bitcast.7) | non-fusion elementwise | flops 147456 | bytes 1769472 | tf_op jit(solution)/shard_map/sub | solution.py:592
  (1 shorter events, 0.0 us)
Async XLA Ops:
  34.7 1.0 %copy-start = (f32[8,60,256]{2,1,0:T(8,128)S(1)}, f32[8,60,256]{2,1,0:T(8,128)}, u32[]{:S(2)}) copy-start(f32[8,60,256]{2,1,0:T(8,128)} %get-tuple-element.10.in_ref) | copy-start | bytes 1474564
  35.7 20.8 %copy-start.2 = (f32[3,8,2048]{2,1,0:T(8,128)S(1)}, f32[3,8,2048]{2,1,0:T(8,128)}, u32[]{:S(2)}) copy-start(f32[3,8,2048]{2,1,0:T(8,128)} %depth_ref.1) | copy-start | bytes 589828
  56.5 1.1 %copy-start.1 = (f32[9,8,2048]{2,1,0:T(8,128)S(1)}, f32[9,8,2048]{2,1,0:T(8,128)}, u32[]{:S(2)}) copy-start(f32[9,8,2048]{2,1,0:T(8,128)} %get-tuple-element.9.adjoint_ref) | copy-start | bytes 1769476
  57.6 23.4 %copy-start.3 = (f32[1,3,3,8,2048]{4,3,2,1,0:T(8,128)S(1)}, f32[1,3,3,8,2048]{4,3,2,1,0:T(8,128)}, u32[]{:S(2)}) copy-start(f32[1,3,3,8,2048]{4,3,2,1,0:T(8,128)} %param.8) | copy-start | bytes 1769476
